TPU v7x, 512 devices: a whole 4x8x8 slice. The times are simulated.
512 devices in a mesh: chan: 16 (over z_lo, x, core), slab: 32 (over y, z_hi).
Axes of the slice: x: 4, y: 8, z: 8 (z_hi: 4, z_lo: 2; z = z_hi * 2 + z_lo), core: 2. Of those that a mesh axis runs over, the one named last changes fastest.
Arguments:
- image: float32 [16, 1024, 1024], P('chan', 'slab'), may hold values from 0 to 2
- margin: int32 [32], P('slab'), may hold values from 1 to 3
- cells: int32 [16, 131072], P('chan', 'slab'), may hold values from 1 to 32767
- weights: float32 [16, 131072], P('chan', 'slab'), may hold values from 0.25 to 4
- observed: float32 [2, 16, 131072], P(None, 'chan', 'slab'), may hold values from -6 to 6
- dual_start: float32 [2, 16, 131072], P(None, 'chan', 'slab'), may hold values from -4 to 4
Outputs:
- restored: float32 [16, 1024, 1024], P('chan', 'slab')
- vis_dual: float32 [2, 16, 131072], P(None, 'chan', 'slab')
Inputs may be any that keep to these rules, and one draw needn't show every extreme that they name: `cells`: visibility k of a channel belongs to facet s = k div 4096; its value q names frequency column s * 32 + q div 1024 and frequency row q mod 1024.
All inputs are finite; a program needn't handle non-finite values.
Results may differ from a plain program's by a relative error of at most 0.0047.
Values may be sent and summed in bfloat16 or wider, within the bound.
No kernel may reach another device: no remote copies, remote signals or barrier semaphores. Data moves between devices by JAX's collectives and lax.ppermute only.
A program may use at most 64 MiB of HBM per device.

v0:
```python
import math

import jax
import jax.numpy as jnp
from jax import lax
from jax.sharding import PartitionSpec as P

N = 1024
HALO = 3


low_taps = (
    -0.010597401784997278,
    0.032883011666982945,
    0.030841381835986965,
    -0.18703481171888114,
    -0.02798376941698385,
    0.6308807679295904,
    0.7148465705525415,
    0.23037781330885523,
)
high_taps = (
    -0.23037781330885523,
    0.7148465705525415,
    -0.6308807679295904,
    -0.02798376941698385,
    0.18703481171888114,
    0.030841381835986965,
    -0.032883011666982945,
    -0.010597401784997278,
)
tau_step = 0.5
bound_level = 3.0
leading = (((0,), (0,)), ((), ()))


def with_halo(block, sides, width):
    for axis, dim in sides:
        count = lax.axis_size(axis)
        forward = [(i, i + 1) for i in range(count - 1)]
        backward = [(target, source) for source, target in forward]
        low = lax.ppermute(
            lax.slice_in_dim(block, block.shape[dim] - width, None, axis=dim), axis, forward
        )
        high = lax.ppermute(lax.slice_in_dim(block, 0, width, axis=dim), axis, backward)
        block = jnp.concatenate([low, block, high], axis=dim)
    return block


def tap_value(offset, taps):
    total = jnp.zeros(offset.shape, jnp.float32)
    for position in range(8):
        total = total + jnp.where(offset == position, taps[position], 0.0).astype(jnp.float32)
    return total


def fourier_tables(length):
    index = jnp.arange(length, dtype=jnp.int32)
    product = index[:, None] * index[None, :] % length
    angle = product.astype(jnp.float32) * (2.0 * math.pi / length)
    scale = 1.0 / math.sqrt(length)
    return (
        (jnp.cos(angle) * scale).astype(jnp.bfloat16),
        (jnp.sin(angle) * scale).astype(jnp.bfloat16),
    )


def row_matrix(count):
    half = count // 2
    line = jnp.arange(count + 2 * HALO, dtype=jnp.int32)[:, None]
    column = jnp.arange(count, dtype=jnp.int32)[None, :]
    offset = line - 2 * (column % half)
    return jnp.where(column < half, tap_value(offset, low_taps), tap_value(offset, high_taps))


def facet_mask(count, width):
    line = jnp.arange(count + 2 * HALO, dtype=jnp.int32)
    distance = jnp.maximum(jnp.maximum(HALO - line, line - count - HALO + 1), 0)
    return (distance[None, :] <= width[:, None]).astype(jnp.float32)


def column_forward(values):
    width = values.shape[1]
    half = width // 2
    padded = jnp.pad(values, ((0, 0), (HALO, 8)))
    even_cells = padded[:, 0::2]
    odd_cells = padded[:, 1::2]
    low_part = jnp.zeros((values.shape[0], half), jnp.float32)
    high_part = jnp.zeros((values.shape[0], half), jnp.float32)
    for position in range(8):
        source = even_cells if position % 2 == 0 else odd_cells
        piece = source[:, position // 2 : position // 2 + half]
        low_part = low_part + low_taps[position] * piece
        high_part = high_part + high_taps[position] * piece
    return jnp.concatenate([low_part, high_part], axis=1)


def column_adjoint(coefs):
    width = coefs.shape[1]
    half = width // 2
    low_part = coefs[:, :half]
    high_part = coefs[:, half:]
    even_sums = jnp.zeros((coefs.shape[0], half + 4), jnp.float32)
    odd_sums = jnp.zeros((coefs.shape[0], half + 4), jnp.float32)
    for position in range(8):
        term = low_taps[position] * low_part + high_taps[position] * high_part
        placed = jnp.pad(term, ((0, 0), (position // 2, 4 - position // 2)))
        if position % 2 == 0:
            even_sums = even_sums + placed
        else:
            odd_sums = odd_sums + placed
    joined = jnp.stack([even_sums, odd_sums], axis=2).reshape(coefs.shape[0], width + 8)
    return joined[:, HALO : HALO + width]


def data_part(lifted, dual, seen, places, gains, cos_table, sin_table):
    flat_b = lifted.astype(jnp.bfloat16)
    spectra = jnp.stack(
        [
            jnp.dot(flat_b, cos_table, preferred_element_type=jnp.float32),
            -jnp.dot(flat_b, sin_table, preferred_element_type=jnp.float32),
        ]
    ).astype(jnp.bfloat16)
    columns = lax.all_to_all(spectra, "slab", split_axis=2, concat_axis=1, tiled=True)
    grid_real = lax.dot_general(
        columns[0], cos_table, leading, preferred_element_type=jnp.float32
    ) + lax.dot_general(columns[1], sin_table, leading, preferred_element_type=jnp.float32)
    grid_imag = lax.dot_general(
        columns[1], cos_table, leading, preferred_element_type=jnp.float32
    ) - lax.dot_general(columns[0], sin_table, leading, preferred_element_type=jnp.float32)
    model = jnp.stack(
        [gains * grid_real.reshape(-1)[places], gains * grid_imag.reshape(-1)[places]]
    )
    fresh_dual = (dual + (model - seen)) / 2.0
    weighted = gains[None, :] * fresh_dual
    cell_count = grid_real.size
    hold_real = (
        jnp.zeros((cell_count,), jnp.float32)
        .at[places]
        .add(weighted[0])
        .reshape(grid_real.shape)
        .astype(jnp.bfloat16)
    )
    hold_imag = (
        jnp.zeros((cell_count,), jnp.float32)
        .at[places]
        .add(weighted[1])
        .reshape(grid_real.shape)
        .astype(jnp.bfloat16)
    )
    backward = jnp.stack(
        [
            jnp.dot(hold_real, cos_table, preferred_element_type=jnp.float32)
            - jnp.dot(hold_imag, sin_table, preferred_element_type=jnp.float32),
            jnp.dot(hold_real, sin_table, preferred_element_type=jnp.float32)
            + jnp.dot(hold_imag, cos_table, preferred_element_type=jnp.float32),
        ]
    ).astype(jnp.bfloat16)
    returned = lax.all_to_all(backward, "slab", split_axis=2, concat_axis=1, tiled=True)
    data_term = lax.dot_general(
        returned[0], cos_table, leading, preferred_element_type=jnp.float32
    ) - lax.dot_general(returned[1], sin_table, leading, preferred_element_type=jnp.float32)
    return (data_term, fresh_dual)


def wave_part(lifted, row_map, mask):
    highest = lax.Precision.HIGHEST
    count = lifted.shape[0]
    extended = with_halo(lifted, (("slab", 0),), HALO) * mask
    filtered = column_forward(extended)
    coef = lax.dot_general(
        row_map, filtered, leading, precision=highest, preferred_element_type=jnp.float32
    )
    squares = coef * coef
    total = lax.psum(squares.astype(jnp.bfloat16), "chan").astype(jnp.float32)
    factor = bound_level / jnp.maximum(jnp.sqrt(total), bound_level)
    fresh_dual = coef * factor
    back = column_adjoint(fresh_dual)
    spread = jnp.dot(row_map, back, precision=highest, preferred_element_type=jnp.float32) * mask
    bands = jnp.concatenate([spread[:HALO], spread[count + HALO :]], axis=0)
    arrived = with_halo(bands, (("slab", 0),), HALO)
    inner = spread[HALO : count + HALO]
    inner = inner.at[:HALO].add(arrived[:HALO])
    inner = inner.at[count - HALO :].add(arrived[3 * HALO :])
    return (inner, fresh_dual)


def local(image, margin, cells, weights, observed, dual_start):
    count = image.shape[1]
    cos_table, sin_table = fourier_tables(N)
    row_map = row_matrix(count)
    mask = facet_mask(count, margin)[0][:, None]
    places = cells[0]
    gains = weights[0]
    seen = observed[:, 0, :]
    dual = dual_start[:, 0, :]
    estimate = image[0]
    data_term, dual = data_part(estimate, dual, seen, places, gains, cos_table, sin_table)
    wave_term, wave_dual = wave_part(estimate, row_map, mask)
    fresh = jnp.maximum(estimate - tau_step * (data_term + wave_term), 0.0)
    return (fresh[None], dual[:, None, :])


def solution(mesh):
    in_specs = (
        P("chan", "slab", None),
        P("slab"),
        P("chan", "slab"),
        P("chan", "slab"),
        P(None, "chan", "slab"),
        P(None, "chan", "slab"),
    )
    out_specs = (P("chan", "slab", None), P(None, "chan", "slab"))
    return jax.shard_map(local, mesh=mesh, in_specs=in_specs, out_specs=out_specs, check_vma=False)
```

profile of v0, /device:TPU:8, one launch (start us, length us, event | category | flops | bytes accessed | tf_op | source)
XLA Modules:
  0.0 495.2 jit_solution(3254002874422707450)
XLA Ops:
  7.2 0.0 copy-start
  7.2 16.8 %fusion.35 = bf16[1,32,1024]{2,1,0:T(8,128)(2,1)S(1)} fusion(f32[1,32,1024]{2,1,0:T(8,128)} %param.10), kind=kOutput, calls=%fused_computation.45 | convolution fusion | flops 83886080 | bytes 196608 | tf_op jit(solution)/shard_map/dot_general | solution.py:120
  24.0 0.0 copy-done
  24.0 16.0 %fusion.36 = bf16[1,32,1024]{2,1,0:T(8,128)(2,1)S(1)} fusion(f32[1,32,1024]{2,1,0:T(8,128)S(1)} %copy-done), kind=kOutput, calls=%fused_computation.46 | convolution fusion | flops 83951616 | bytes 196608 | tf_op jit(solution)/shard_map/dot_general | solution.py:121
  40.0 0.4 copy.11
  40.4 1.2 reshape.188
  41.6 16.2 %all-to-all-start = ((bf16[32,2,1024]{2,1,0:T(2,128)(2,1)}), bf16[32,2,1024]{2,1,0:T(2,128)(2,1)S(1)}, u32[]{:S(2)}, u32[]{:S(2)}) async-start(bf16[32,2,1024]{2,1,0:T(2,128)(2,1)} %reshape.188), calls=%async_computation | async-start | bytes 262144 | tf_op jit(solution)/shard_map/all_to_all | solution.py:124
  57.8 0.0 all-reduce.11.cloned.1.call-start
  57.8 4.3 collective-permute-start
  62.1 4.8 collective-permute-start.1
  67.6 0.0 collective-permute-done
  67.6 1.8 collective-permute-done.1
  69.4 0.1 maximum_multiply_fusion
  69.5 0.1 pad.36
  69.6 2.7 slice.133
  72.2 2.7 slice.135
  74.9 0.0 copy-start.3
  74.9 0.2 multiply_add_fusion.1
  75.1 1.0 multiply_convert_fusion.56
  76.1 0.0 all-reduce.11.cloned.1.call-update
  76.2 116.7 %all-reduce.11.cloned.1.call-done = bf16[32,1024]{1,0:T(8,128)(2,1)} async-done(((bf16[32,1024]{1,0:T(8,128)(2,1)}), bf16[32,1024]{1,0:T(8,128)(2,1)}) %all-reduce.11.cloned.1.call-update) | async-done | bytes 65552 | tf_op jit(solution)/shard_map/psum | solution.py:175
  192.9 0.9 divide_multiply_fusion
  193.8 0.1 multiply_add_fusion.9
  193.8 0.2 add_bitcast_fusion
  194.1 0.3 copy.15
  194.3 0.7 convolution_multiply_fusion
  195.0 4.6 collective-permute-start.2
  199.7 4.6 collective-permute-start.3
  204.3 0.0 collective-permute-done.2
  204.4 0.3 scatter-add.26
  204.7 2.7 collective-permute-done.3
  207.4 0.2 scatter-add.27
  207.6 0.0 all-to-all-done
  207.6 0.3 reshape.189
  207.9 0.3 copy.25
  208.3 0.3 squeeze.37
  208.6 15.9 %fusion.9 = f32[32,1024]{1,0:T(8,128)S(1)} fusion(bf16[1024,32]{0,1:T(8,128)(2,1)S(1)} %squeeze.37), kind=kOutput, calls=%fused_computation.18 | convolution fusion | flops 83886080 | bytes 196608 | tf_op jit(solution)/shard_map/dot_general | solution.py:128
  224.4 0.3 squeeze.36
  224.7 15.9 %fusion.10 = f32[32,1024]{1,0:T(8,128)S(1)} fusion(bf16[1024,32]{0,1:T(8,128)(2,1)S(1)} %squeeze.36), kind=kOutput, calls=%fused_computation.19 | convolution fusion | flops 83886080 | bytes 196608 | tf_op jit(solution)/shard_map/dot_general | solution.py:125
  240.6 16.2 %fusion.22 = f32[4,8,8,128]{3,2,1,0:T(8,128)S(1)} fusion(f32[32,1024]{1,0:T(8,128)S(1)} %fusion.9, bf16[1024,32]{0,1:T(8,128)(2,1)S(1)} %squeeze.36), kind=kOutput, calls=%fused_computation.32 | convolution fusion | flops 83918848 | bytes 327680 | tf_op jit(solution)/shard_map/dot_general | solution.py:130
  256.8 16.0 %fusion.20 = f32[4,8,8,128]{3,2,1,0:T(8,128)S(1)} fusion(f32[32,1024]{1,0:T(8,128)S(1)} %fusion.10, bf16[1024,32]{0,1:T(8,128)(2,1)S(1)} %squeeze.37), kind=kOutput, calls=%fused_computation.30 | convolution fusion | flops 83918848 | bytes 327680 | tf_op jit(solution)/shard_map/dot_general | solution.py:127
  272.8 23.0 %gather_fusion.1 = f32[4096]{0:T(1024)S(1)} fusion(f32[32768]{0:T(1024)S(1)} %bitcast.111, s32[4096]{0:T(1024)S(1)} %broadcast_clamp_fusion), kind=kCustom, calls=%fused_computation.1 | custom fusion | bytes 49152 | tf_op jit(solution)/shard_map/gather | solution.py:132
  295.9 0.0 copy-start.4
  295.9 0.0 copy-start.1
  295.9 0.0 copy-start.2
  295.9 23.0 %gather_fusion = f32[4096]{0:T(1024)S(1)} fusion(f32[32768]{0:T(1024)S(1)} %bitcast.112, s32[4096]{0:T(1024)S(1)} %broadcast_clamp_fusion), kind=kCustom, calls=%fused_computation | custom fusion | bytes 49152 | tf_op jit(solution)/shard_map/gather | solution.py:132
  319.0 0.1 fusion.49
  319.2 21.9 %scatter_custom_fusion = f32[32768]{0:T(1024)S(1)} fusion(s32[4096]{0:T(1024)S(1)} %bitcast.124, f32[4096]{0:T(1024)S(1)} %bitcast.130, f32[]{:T(128)} %constant.146.clone.1), kind=kCustom, calls=%fused_computation.77 | custom fusion | flops 4096 | bytes 131076 | tf_op jit(solution)/shard_map/scatter-add | solution.py:140
  341.2 16.1 %fusion.8 = f32[32,1024]{1,0:T(8,128)S(1)} fusion(bf16[32,1024]{1,0:T(8,128)(2,1)S(1)} %convert_element_type.102), kind=kOutput, calls=%fused_computation.17 | convolution fusion | flops 83886080 | bytes 196608 | tf_op jit(solution)/shard_map/dot_general | solution.py:153
  357.3 21.9 %scatter_custom_fusion.1 = f32[32768]{0:T(1024)S(1)} fusion(s32[4096]{0:T(1024)S(1)} %bitcast.125, f32[4096]{0:T(1024)S(1)} %bitcast.129, f32[]{:T(128)} %constant.146.clone.1), kind=kCustom, calls=%fused_computation.75 | custom fusion | flops 4096 | bytes 131076 | tf_op jit(solution)/shard_map/scatter-add | solution.py:147
  379.3 15.9 %fusion.7 = f32[32,1024]{1,0:T(8,128)S(1)} fusion(bf16[32,1024]{1,0:T(8,128)(2,1)S(1)} %convert_element_type.104), kind=kOutput, calls=%fused_computation.16 | convolution fusion | flops 83886080 | bytes 196608 | tf_op jit(solution)/shard_map/dot_general | solution.py:156
  395.2 16.8 %fusion.37 = bf16[1,32,1024]{2,1,0:T(8,128)(2,1)S(1)} fusion(f32[32,1024]{1,0:T(8,128)S(1)} %fusion.8, bf16[32,1024]{1,0:T(8,128)(2,1)S(1)} %convert_element_type.104), kind=kOutput, calls=%fused_computation.47 | convolution fusion | flops 83951616 | bytes 262144 | tf_op jit(solution)/shard_map/dot_general | solution.py:154
  411.9 16.8 %fusion.38 = bf16[1,32,1024]{2,1,0:T(8,128)(2,1)S(1)} fusion(f32[32,1024]{1,0:T(8,128)S(1)} %fusion.7, bf16[32,1024]{1,0:T(8,128)(2,1)S(1)} %convert_element_type.102), kind=kOutput, calls=%fused_computation.48 | convolution fusion | flops 83951616 | bytes 262144 | tf_op jit(solution)/shard_map/dot_general | solution.py:155
  428.7 0.4 copy.13
  429.1 1.2 reshape.190
  430.3 11.2 %all-to-all-start.1 = ((bf16[32,2,1024]{2,1,0:T(2,128)(2,1)}), bf16[32,2,1024]{2,1,0:T(2,128)(2,1)S(1)}, u32[]{:S(2)}, u32[]{:S(2)}) async-start(bf16[32,2,1024]{2,1,0:T(2,128)(2,1)} %reshape.190), calls=%async_computation.1 | async-start | bytes 262144 | tf_op jit(solution)/shard_map/all_to_all | solution.py:159
  441.5 0.7 fusion.53
  442.2 11.1 %all-to-all-done.1 = bf16[32,2,1024]{2,1,0:T(2,128)(2,1)S(1)} async-done(((bf16[32,2,1024]{2,1,0:T(2,128)(2,1)}), bf16[32,2,1024]{2,1,0:T(2,128)(2,1)S(1)}, u32[]{:S(2)}, u32[]{:S(2)}) %all-to-all-start.1) | async-done | bytes 131104 | tf_op jit(solution)/shard_map/all_to_all | solution.py:159
  453.4 0.3 reshape.191
  453.6 0.3 copy.24
  454.0 0.3 squeeze.41
  454.3 15.9 %fusion.6 = f32[32,1024]{1,0:T(8,128)S(1)} fusion(bf16[1024,32]{0,1:T(8,128)(2,1)S(1)} %squeeze.41), kind=kOutput, calls=%fused_computation.15 | convolution fusion | flops 83886080 | bytes 196608 | tf_op jit(solution)/shard_map/dot_general | solution.py:160
  470.2 0.3 squeeze.42
  470.5 17.4 %fusion.30 = f32[1,32,1024]{2,1,0:T(8,128)} fusion(f32[32,1024]{1,0:T(8,128)S(1)} %scatter-add.27, f32[32,1024]{1,0:T(8,128)S(1)} %fusion.6, bf16[1024,32]{0,1:T(8,128)(2,1)S(1)} %squeeze.42, f32[1,32,1024]{2,1,0:T(8,128)S(1)} %copy-done), kind=kOutput, calls=%fused_computation.40 | convolution fusion | flops 84049920 | bytes 589824 | tf_op jit(solution)/shard_map/dot_general | solution.py:162
  (27 shorter events, 0.4 us)
Async XLA Ops:
  7.2 16.8 %copy-start = (f32[1,32,1024]{2,1,0:T(8,128)S(1)}, f32[1,32,1024]{2,1,0:T(8,128)}, u32[]{:S(2)}) copy-start(f32[1,32,1024]{2,1,0:T(8,128)} %param.10) | copy-start | bytes 393220
  41.6 166.0 %all-to-all-start = ((bf16[32,2,1024]{2,1,0:T(2,128)(2,1)}), bf16[32,2,1024]{2,1,0:T(2,128)(2,1)S(1)}, u32[]{:S(2)}, u32[]{:S(2)}) async-start(bf16[32,2,1024]{2,1,0:T(2,128)(2,1)} %reshape.188), calls=%async_computation | async-start | bytes 262144 | tf_op jit(solution)/shard_map/all_to_all | solution.py:124
  57.8 135.1 %all-reduce.11.cloned.1.call-start = ((), (), s32[]{:S(2)}) async-start(), calls=%async_computation.2 | async-start | bytes 131072 | tf_op jit(solution)/shard_map/psum | solution.py:175
  57.8 9.8 %collective-permute-start = (f32[3,1024]{1,0:T(4,128)S(1)}, f32[3,1024]{1,0:T(4,128)S(1)}, u32[]{:S(2)}, u32[]{:S(2)}) collective-permute-start(f32[3,1024]{1,0:T(4,128)S(1)} %get-tuple-element.42), channel_id=1, source_target_pairs={{0,1},{1,2},{2,3},{3,4},{4,5},{5,6},{6,7},{7,8},{8,9},{9,10},{10,1... | collective-permute-start | bytes 36872 | tf_op jit(solution)/shard_map/ppermute | solution.py:42
  62.1 7.3 %collective-permute-start.1 = (f32[3,1024]{1,0:T(4,128)S(1)}, f32[3,1024]{1,0:T(4,128)S(1)}, u32[]{:S(2)}, u32[]{:S(2)}) collective-permute-start(f32[3,1024]{1,0:T(4,128)S(1)} %get-tuple-element.43), channel_id=1, source_target_pairs={{1,0},{2,1},{3,2},{4,3},{5,4},{6,5},{7,6},{8,7},{9,8},{10,9},{11,1... | collective-permute-start | bytes 36872 | tf_op jit(solution)/shard_map/ppermute | solution.py:45
  74.9 1.2 copy-start.3
  195.0 9.3 %collective-permute-start.2 = (f32[3,1024]{1,0:T(4,128)S(1)}, f32[3,1024]{1,0:T(4,128)S(1)}, u32[]{:S(2)}, u32[]{:S(2)}) collective-permute-start(f32[3,1024]{1,0:T(4,128)S(1)} %get-tuple-element.33), channel_id=1, source_target_pairs={{0,1},{1,2},{2,3},{3,4},{4,5},{5,6},{6,7},{7,8},{8,9},{9,10},{10,1... | collective-permute-start | bytes 36872 | tf_op jit(solution)/shard_map/ppermute | solution.py:42
  199.7 7.7 %collective-permute-start.3 = (f32[3,1024]{1,0:T(4,128)S(1)}, f32[3,1024]{1,0:T(4,128)S(1)}, u32[]{:S(2)}, u32[]{:S(2)}) collective-permute-start(f32[3,1024]{1,0:T(4,128)S(1)} %get-tuple-element.32), channel_id=1, source_target_pairs={{1,0},{2,1},{3,2},{4,3},{5,4},{6,5},{7,6},{8,7},{9,8},{10,9},{11,1... | collective-permute-start | bytes 36872 | tf_op jit(solution)/shard_map/ppermute | solution.py:45
  295.9 23.1 %copy-start.4 = (f32[1,4096]{1,0:T(1,128)S(1)}, f32[1,4096]{1,0:T(1,128)}, u32[]{:S(2)}) copy-start(f32[1,4096]{1,0:T(1,128)} %param.13) | copy-start | bytes 49156
  295.9 23.1 %copy-start.1 = (f32[2,1,4096]{2,1,0:T(1,128)S(1)}, f32[2,1,4096]{2,1,0:T(1,128)}, u32[]{:S(2)}) copy-start(f32[2,1,4096]{2,1,0:T(1,128)} %param.14) | copy-start | bytes 98308
  295.9 23.1 %copy-start.2 = (f32[2,1,4096]{2,1,0:T(1,128)S(1)}, f32[2,1,4096]{2,1,0:T(1,128)}, u32[]{:S(2)}) copy-start(f32[2,1,4096]{2,1,0:T(1,128)} %param.15) | copy-start | bytes 98308
  430.3 23.1 %all-to-all-start.1 = ((bf16[32,2,1024]{2,1,0:T(2,128)(2,1)}), bf16[32,2,1024]{2,1,0:T(2,128)(2,1)S(1)}, u32[]{:S(2)}, u32[]{:S(2)}) async-start(bf16[32,2,1024]{2,1,0:T(2,128)(2,1)} %reshape.190), calls=%async_computation.1 | async-start | bytes 262144 | tf_op jit(solution)/shard_map/all_to_all | solution.py:159
Sparse Core Ops, SparseCore 0:
  76.2 116.5 all-reduce.10
where the time goes:
time: 502 us; the launch traced here: 495 us
  matrix products  197 us (39%)
  waiting for transfers between devices  132 us (26%)
  local copies, waits for them, and re-layouts  58 us (12%)
  other arithmetic  46.2 us (9%)
  starting transfers between devices  45.8 us (9%)
  between operations  15.7 us (3%)
    psum x1, waiting for transfers between devices, wave_part(): total = lax.psum(squares.astype(jnp.bfloat16), 'chan').astype(jnp.float32)  117 us
    gather x1, local copies, waits for them, and re-layouts, data_part(): grid_imag.reshape(-1)[places]  23 us
    gather x1, local copies, waits for them, and re-layouts, data_part(): grid_real.reshape(-1)[places]  23 us
    scatter-add x1, other arithmetic, data_part(): hold_real = jnp.zeros((cell_count,), jnp.float32).at[places].add(weighted...  21.9 us
    scatter-add x1, other arithmetic, data_part(): hold_imag = jnp.zeros((cell_count,), jnp.float32).at[places].add(weighted...  21.9 us
    dot_general x1, matrix products, data_part(): lax.dot_general(returned[1], sin_table, leading, preferred_element_type=j...  17.4 us
    dot_general x1, matrix products, data_part(): jnp.dot(flat_b, cos_table, preferred_element_type=jnp.float32)  16.8 us
    dot_general x1, matrix products, data_part(): jnp.dot(hold_imag, sin_table, preferred_element_type=jnp.float32)  16.8 us
  transfers between devices with their start and end apart: 7, of which 4 were waited for; matrix products, arithmetic and copies ran while one was open for 2% of the time, Pallas kernels for 0%

commit v1 on v0

v1 whole, which is shorter than its diff:
```python
import math

import jax
import jax.numpy as jnp
import numpy as np
from jax import lax
from jax.experimental import pallas as pl
from jax.experimental.pallas import tpu as pltpu
from jax.sharding import PartitionSpec as P

N = 1024
ROWS = 32
FACETS = 32
CHANNELS = 16
VIS = 4096
STEP = 512

low_taps = (
    -0.010597401784997278,
    0.032883011666982945,
    0.030841381835986965,
    -0.18703481171888114,
    -0.02798376941698385,
    0.6308807679295904,
    0.7148465705525415,
    0.23037781330885523,
)
high_taps = (
    -0.23037781330885523,
    0.7148465705525415,
    -0.6308807679295904,
    -0.02798376941698385,
    0.18703481171888114,
    0.030841381835986965,
    -0.032883011666982945,
    -0.010597401784997278,
)
tau_step = 0.5
bound_level = 3.0
f32 = jnp.float32
bf16 = jnp.bfloat16


def tap_of(position, line):
    offset = line - position
    if position % 2 == 0:
        return low_taps[offset + 3] if 0 <= offset + 3 < 8 else 0.0
    return high_taps[offset + 4] if 0 <= offset + 4 < 8 else 0.0


def fourier_tables():
    index = np.arange(N, dtype=np.int32)
    product = index[:, None] * index[None, :] % N
    angle = product.astype(np.float32) * np.float32(2.0 * math.pi / N)
    scale = np.float32(1.0 / math.sqrt(N))
    shape = (FACETS, 2, 16, N)
    return (
        (np.cos(angle) * scale).astype(bf16).reshape(shape),
        (np.sin(angle) * scale).astype(bf16).reshape(shape),
    )


def column_weights():
    forward = np.zeros((16, N), np.float32)
    adjoint = np.zeros((16, N), np.float32)
    for shift in range(-4, 5):
        for n in range(N):
            if 0 <= n + shift < N:
                forward[shift + 4, n] = tap_of(n % 2, n % 2 + shift)
                source = n + shift
                adjoint[shift + 4, n] = tap_of(source % 2, source % 2 - shift)
    return forward, adjoint


def row_weights():
    taps = np.zeros((48, 48), np.float32)
    distance = np.zeros((48, 48), np.float32)
    for a in range(40):
        for b in range(48):
            position, line = a - 4, b - 8
            taps[a, b] = tap_of(position, line)
            if position < 0:
                distance[a, b] = max(line + 1, 0)
            elif position < ROWS:
                distance[a, b] = max(-line, line - ROWS + 1, 0)
            else:
                distance[a, b] = max(ROWS - line, 0)
    return taps, distance


def exchange_groups(groups):
    lane = lax.broadcasted_iota(jnp.int32, groups[0].shape, 1)
    g = list(groups)
    for width, pairs in ((64, ((0, 2), (1, 3))), (32, ((0, 1), (2, 3)))):
        first = (lane % (2 * width)) < width
        for a, b in pairs:
            x, y = g[a], g[b]
            g[a] = jnp.where(first, x, pltpu.roll(y, width, 1))
            g[b] = jnp.where(first, pltpu.roll(x, 128 - width, 1), y)
    return g


def pack(real, imag, out_ref):
    for block in range(8):
        span = slice(128 * block, 128 * (block + 1))
        groups = [real[:16, span], real[16:, span], imag[:16, span], imag[16:, span]]
        for d, chunk in enumerate(exchange_groups(groups)):
            out_ref[4 * block + d] = chunk.astype(bf16)


def dot(a, b):
    return jnp.dot(a, b, preferred_element_type=f32)


def forward_kernel(image_ref, cos_ref, sin_ref, out_ref):
    flat = image_ref[0].astype(bf16)
    real = dot(flat, cos_ref[...].reshape(N, N))
    imag = -dot(flat, sin_ref[...].reshape(N, N))
    pack(real, imag, out_ref)


def vis_kernel(
    got_ref, cells_ref, gains_ref, seen_ref, dual_ref, cos_ref, sin_ref, dual_out, out_ref
):
    turned = got_ref[...].reshape(512, 128).T
    by_cos = jnp.zeros((64, N), f32)
    by_sin = jnp.zeros((64, N), f32)
    for h in range(2):
        left = jnp.concatenate(
            [turned[32 * h : 32 * h + 32], turned[64 + 32 * h : 96 + 32 * h]], axis=0
        )
        by_cos = by_cos + dot(left, cos_ref[:, h].reshape(512, N))
        by_sin = by_sin + dot(left, sin_ref[:, h].reshape(512, N))
    grid = (by_cos[:32] + by_sin[32:], by_cos[32:] - by_sin[:32])
    stacked = jnp.concatenate(
        [part[:, 256 * t : 256 * t + 256] for part in grid for t in range(4)], axis=0
    )
    upper = stacked.astype(bf16)
    lower = (stacked - upper.astype(f32)).astype(bf16)
    lines = jnp.concatenate([upper, lower], axis=1)
    cell_lane = lax.broadcasted_iota(jnp.int32, (256, STEP), 0)
    cell_line = lax.broadcasted_iota(jnp.int32, (128, STEP), 0)
    hold = jnp.zeros((256, 256), f32)
    for step in range(VIS // STEP):
        span = slice(STEP * step, STEP * (step + 1))
        cell = cells_ref[:, span]
        lane = cell & 255
        line = ((cell >> 8) & 3) * 32 + (cell >> 10)
        gains = gains_ref[:, span]
        here = jnp.where(cell_lane == lane, 1.0, 0.0).astype(bf16)
        chosen = cell_line == line
        values = dot(lines, jnp.concatenate([here, here], axis=0))
        spread = []
        for c in range(2):
            picked = jnp.sum(
                jnp.where(chosen, values[128 * c : 128 * c + 128], 0.0), axis=0, keepdims=True
            )
            fresh = (dual_ref[c, :, span] + (gains * picked - seen_ref[c, :, span])) / 2.0
            dual_out[c, :, span] = fresh
            spread.append(jnp.where(chosen, gains * fresh, 0.0).astype(bf16))
        hold = hold + lax.dot_general(
            jnp.concatenate(spread, axis=0),
            here,
            (((1,), (1,)), ((), ())),
            preferred_element_type=f32,
        )
    held = hold.astype(bf16)
    held = jnp.concatenate(
        [
            jnp.concatenate(
                [held[128 * c + 32 * t : 128 * c + 32 * t + 32] for t in range(4)], axis=1
            )
            for c in range(2)
        ],
        axis=0,
    )
    by_cos = dot(held, cos_ref[...].reshape(N, N))
    by_sin = dot(held, sin_ref[...].reshape(N, N))
    pack(by_cos[:32] - by_sin[32:], by_sin[:32] + by_cos[32:], out_ref)


def filtered_columns(values, weights_ref):
    total = values * weights_ref[4:5, :]
    for shift in range(-4, 5):
        if shift:
            moved = pltpu.roll(values, (-shift) % N, 1)
            total = total + moved * weights_ref[shift + 4 : shift + 5, :]
    return total


def exact_dot(a, b, dims):
    return lax.dot_general(
        a, b, (dims, ((), ())), precision=lax.Precision.HIGHEST, preferred_element_type=f32
    )


def wave_kernel(
    margin_ref, image_ref, low_ref, high_ref, taps_ref, dist_ref, weights_ref,
    coef_ref, square_ref, rows_ref,
):
    own = margin_ref[0].astype(f32)
    place = lax.broadcasted_iota(jnp.int32, (48, 48), 0)
    above = jnp.broadcast_to(low_ref[0:1, 0:48], (48, 48))
    below = jnp.broadcast_to(high_ref[7:8, 0:48], (48, 48))
    width = jnp.where(place < 4, above, jnp.where(place < 36, own, below))
    rows = jnp.where(dist_ref[...] <= width, taps_ref[...], 0.0)
    rows_ref[...] = rows
    extended = jnp.concatenate([low_ref[...], image_ref[0], high_ref[...]], axis=0)
    coef = filtered_columns(exact_dot(rows, extended, ((1,), (0,))), weights_ref)
    coef_ref[...] = coef
    square = (coef * coef).astype(bf16)
    for block in range(8):
        for half in range(2):
            square_ref[2 * block + half] = square[
                24 * half : 24 * half + 24, 128 * block : 128 * block + 128
            ]


def total_kernel(parts_ref, out_ref):
    total = jnp.sum(parts_ref[...].astype(f32), axis=0).astype(bf16)
    out_ref[...] = jnp.broadcast_to(total[None], out_ref.shape)


def back_kernel(coef_ref, total_ref, rows_ref, weights_ref, out_ref):
    pieces = []
    for half in range(2):
        pieces.append(
            jnp.concatenate(
                [total_ref[2 * block + half].astype(f32) for block in range(8)], axis=1
            )
        )
    total = jnp.concatenate(pieces, axis=0)
    factor = bound_level / jnp.maximum(jnp.sqrt(total), bound_level)
    mixed = exact_dot(rows_ref[...], coef_ref[...] * factor, ((0,), (0,)))
    out_ref[...] = filtered_columns(mixed[8:40], weights_ref)


def final_kernel(got_ref, image_ref, wave_ref, cos_ref, sin_ref, out_ref):
    turned = got_ref[...].reshape(512, 128).T
    total = wave_ref[...]
    for h in range(2):
        total = total + dot(turned[32 * h : 32 * h + 32], cos_ref[:, h].reshape(512, N))
        total = total - dot(turned[64 + 32 * h : 96 + 32 * h], sin_ref[:, h].reshape(512, N))
    out_ref[0] = jnp.maximum(image_ref[0] - tau_step * total, 0.0)


params = pltpu.CompilerParams(vmem_limit_bytes=48 * 1024 * 1024)
in_vmem = pl.BlockSpec(memory_space=pltpu.VMEM)
in_smem = pl.BlockSpec(memory_space=pltpu.SMEM)


def call(kernel, name, out_shape, *args, specs=None):
    return pl.pallas_call(
        kernel,
        out_shape=out_shape,
        in_specs=specs or [in_vmem] * len(args),
        out_specs=jax.tree.map(lambda _: in_vmem, out_shape),
        compiler_params=params,
        name=name,
    )(*args)


def shape(dims, kind):
    return jax.ShapeDtypeStruct(dims, kind)


def local(image, margin, cells, weights, observed, dual_start):
    cos_table, sin_table = (jnp.asarray(t) for t in fourier_tables())
    forward_weights, adjoint_weights = (jnp.asarray(t) for t in column_weights())
    taps, distance = (jnp.asarray(t) for t in row_weights())
    chunks = shape((FACETS, 16, 128), bf16)
    squares = shape((CHANNELS, 24, 128), bf16)
    wide = jnp.broadcast_to(margin.astype(f32)[:, None], (1, N))
    up = [(i, i + 1) for i in range(FACETS - 1)]
    down = [(i + 1, i) for i in range(FACETS - 1)]
    low = lax.ppermute(jnp.concatenate([wide, image[0, 25:]], axis=0), "slab", up)
    high = lax.ppermute(jnp.concatenate([image[0, :7], wide], axis=0), "slab", down)
    sent = call(forward_kernel, "rows_out", chunks, image, cos_table, sin_table)
    got = lax.all_to_all(sent, "slab", 0, 0, tiled=True)
    coef, square, rows = call(
        wave_kernel,
        "wave_out",
        (shape((48, N), f32), squares, shape((48, 48), f32)),
        margin, image, low, high, taps, distance, forward_weights,
        specs=[in_smem] + [in_vmem] * 6,
    )
    parts = lax.all_to_all(square, "chan", 0, 0, tiled=True)
    copies = call(total_kernel, "wave_sum", squares, parts)
    totals = lax.all_to_all(copies, "chan", 0, 0, tiled=True)
    wave = call(
        back_kernel, "wave_back", shape((ROWS, N), f32), coef, totals, rows, adjoint_weights
    )
    dual, back = call(
        vis_kernel,
        "visibilities",
        (shape((2, 1, VIS), f32), chunks),
        got, cells, weights, observed, dual_start, cos_table, sin_table,
    )
    returned = lax.all_to_all(back, "slab", 0, 0, tiled=True)
    fresh = call(
        final_kernel, "image_out", shape((1, ROWS, N), f32),
        returned, image, wave, cos_table, sin_table,
    )
    return (fresh, dual)


def solution(mesh):
    in_specs = (
        P("chan", "slab", None),
        P("slab"),
        P("chan", "slab"),
        P("chan", "slab"),
        P(None, "chan", "slab"),
        P(None, "chan", "slab"),
    )
    out_specs = (P("chan", "slab", None), P(None, "chan", "slab"))
    return jax.shard_map(local, mesh=mesh, in_specs=in_specs, out_specs=out_specs, check_vma=False)
```

time: 502 us -> 91.1 us (0.18)
  the two profiles are of different devices: /device:TPU:8 before, /device:TPU:10 now
where the time goes in v1:
time: 91.1 us; the launch traced here: 90.2 us
  starting transfers between devices  40 us (44%)
  waiting for transfers between devices  26.3 us (29%)
  local copies, waits for them, and re-layouts  11.3 us (12%)
  Pallas kernels  11.2 us (12%)
  between operations  1.41 us (2%)
    all_to_all x1, waiting for transfers between devices, local(): returned = lax.all_to_all(back, 'slab', 0, 0, tiled=True)  12.1 us
    all_to_all x1, starting transfers between devices, local(): got = lax.all_to_all(sent, 'slab', 0, 0, tiled=True)  11.9 us
    all_to_all x1, waiting for transfers between devices, local(): got = lax.all_to_all(sent, 'slab', 0, 0, tiled=True)  11.6 us
    pallas_call x6, Pallas kernels, call(): pl.pallas_call(kernel, out_shape=out_shape, in_specs=specs or [in_vmem] *...  11.2 us
    unnamed x32, local copies, waits for them, and re-layouts  10.5 us
    ppermute x1, starting transfers between devices, local(): lax.ppermute(jnp.concatenate([image[0, :7], wide], axis=0), 'slab', down)  6.66 us
    ppermute x1, starting transfers between devices, local(): lax.ppermute(jnp.concatenate([wide, image[0, 25:]], axis=0), 'slab', up)  6.09 us
    all_to_all x1, starting transfers between devices, local(): totals = lax.all_to_all(copies, 'chan', 0, 0, tiled=True)  5.72 us
  transfers between devices with their start and end apart: 6, of which 4 were waited for; matrix products, arithmetic and copies ran while one was open for 0% of the time, Pallas kernels for 9%

profile of v1, /device:TPU:10, one launch (start us, length us, event | category | flops | bytes accessed | tf_op | source)
XLA Modules:
  0.0 90.2 jit_solution(15995210427857944974)
XLA Ops:
  1.3 0.8 slice_bitcast_fusion
  2.1 6.1 %collective-permute-start = (f32[8,1024]{1,0:T(8,128)S(1)}, f32[8,1024]{1,0:T(8,128)S(1)}, u32[]{:S(2)}, u32[]{:S(2)}) collective-permute-start(f32[8,1024]{1,0:T(8,128)S(1)} %concatenate.6), channel_id=1, source_target_pairs={{0,1},{1,2},{2,3},{3,4},{4,5},{5,6},{6,7},{7,8},{8,9},{9,10},{10,1... | collective-permute-start | bytes 98312 | tf_op jit(solution)/shard_map/ppermute | solution.py:276
  8.2 6.7 %collective-permute-start.1 = (f32[8,1024]{1,0:T(8,128)S(1)}, f32[8,1024]{1,0:T(8,128)S(1)}, u32[]{:S(2)}, u32[]{:S(2)}) collective-permute-start(f32[8,1024]{1,0:T(8,128)S(1)} %concatenate.7), channel_id=1, source_target_pairs={{1,0},{2,1},{3,2},{4,3},{5,4},{6,5},{7,6},{8,7},{9,8},{10,9},{11,1... | collective-permute-start | bytes 98312 | tf_op jit(solution)/shard_map/ppermute | solution.py:277
  14.9 0.3 collective-permute-done.low_ref
  15.1 2.4 %collective-permute-done.1.high_ref = f32[8,1024]{1,0:T(8,128)S(1)} collective-permute-done((f32[8,1024]{1,0:T(8,128)S(1)}, f32[8,1024]{1,0:T(8,128)S(1)}, u32[]{:S(2)}, u32[]{:S(2)}) %collective-permute-start.1) | collective-permute-done | bytes 32800 | tf_op jit(solution)/shard_map/ppermute | solution.py:277
  17.5 0.0 copy-start.5
  17.5 0.9 %copy-done.5 = f32[1,32,1024]{2,1,0:T(8,128)S(1)} copy-done((f32[1,32,1024]{2,1,0:T(8,128)S(1)}, f32[1,32,1024]{2,1,0:T(8,128)}, u32[]{:S(2)}) %copy-start.5) | copy-done | bytes 131096
  18.4 0.0 copy-start.8
  18.4 0.8 copy-done.8
  19.2 0.0 copy-start.12
  19.2 0.7 copy-done.12
  20.0 0.0 copy-start.13
  20.0 0.7 copy-done.13
  20.7 1.4 %wave_out.1 = (f32[48,1024]{1,0:T(8,128)S(1)}, bf16[16,24,128]{2,1,0:T(8,128)(2,1)}, f32[48,48]{1,0:T(8,128)S(1)}) custom-call(s32[1]{0:T(128)S(6)} %copy.14.margin_ref, f32[1,32,1024]{2,1,0:T(8,128)S(1)} %copy-done.5, f32[8,1024]{1,0:T(8,128)S(1)} %collective-permute-done.low_ref, f32[8,1024]{1,0:T(8,128)S(1)} %collective-permute-done.1.high_ref, ...), custom_call_target="tpu_custom_call" | custom-call | tf_op jit(solution)/shard_map/wave_out/pallas_call | solution.py:253
  22.1 5.6 %all-to-all-start.2 = ((bf16[16,24,128]{2,1,0:T(8,128)(2,1)}), bf16[16,24,128]{2,1,0:T(8,128)(2,1)S(1)}, u32[]{:S(2)}, u32[]{:S(2)}) async-start(bf16[16,24,128]{2,1,0:T(8,128)(2,1)} %get-tuple-element.9), calls=%async_computation.2 | async-start | bytes 196608 | tf_op jit(solution)/shard_map/all_to_all | solution.py:287
  27.7 0.0 copy-start
  27.7 1.6 %copy-done = bf16[32,2,16,1024]{3,2,1,0:T(8,128)(2,1)S(1)} copy-done((bf16[32,2,16,1024]{3,2,1,0:T(8,128)(2,1)S(1)}, bf16[32,2,16,1024]{3,2,1,0:T(8,128)(2,1)}, u32[]{:S(2)}) %copy-start) | copy-done | bytes 2097176
  29.3 0.0 copy-start.2
  29.3 1.6 %copy-done.2 = bf16[32,2,16,1024]{3,2,1,0:T(8,128)(2,1)S(1)} copy-done((bf16[32,2,16,1024]{3,2,1,0:T(8,128)(2,1)S(1)}, bf16[32,2,16,1024]{3,2,1,0:T(8,128)(2,1)}, u32[]{:S(2)}) %copy-start.2) | copy-done | bytes 2097176
  30.9 0.0 copy-start.6
  30.9 0.9 copy-done.6
  31.8 0.0 copy-start.1
  31.8 0.0 copy-start.10
  31.8 0.0 copy-start.11
  31.8 0.0 copy-start.14
  31.8 0.0 copy-start.15
  31.8 1.6 %rows_out.1 = bf16[32,16,128]{2,1,0:T(8,128)(2,1)} custom-call(f32[1,32,1024]{2,1,0:T(8,128)S(1)} %copy-done.6, bf16[32,2,16,1024]{3,2,1,0:T(8,128)(2,1)S(1)} %copy-done, bf16[32,2,16,1024]{3,2,1,0:T(8,128)(2,1)S(1)} %copy-done.2), custom_call_target="tpu_custom_call" | custom-call | tf_op jit(solution)/shard_map/rows_out/pallas_call | solution.py:253
  33.5 0.0 all-to-all-done.2.parts_ref
  33.5 11.9 %all-to-all-start = ((bf16[32,16,128]{2,1,0:T(8,128)(2,1)}), bf16[32,16,128]{2,1,0:T(8,128)(2,1)S(1)}, u32[]{:S(2)}, u32[]{:S(2)}) async-start(bf16[32,16,128]{2,1,0:T(8,128)(2,1)} %rows_out.1), calls=%async_computation | async-start | bytes 262144 | tf_op jit(solution)/shard_map/all_to_all | solution.py:279
  45.3 0.7 wave_sum.1
  46.0 11.6 %all-to-all-done.got_ref = bf16[32,16,128]{2,1,0:T(8,128)(2,1)S(1)} async-done(((bf16[32,16,128]{2,1,0:T(8,128)(2,1)}), bf16[32,16,128]{2,1,0:T(8,128)(2,1)S(1)}, u32[]{:S(2)}, u32[]{:S(2)}) %all-to-all-start) | async-done | bytes 131104 | tf_op jit(solution)/shard_map/all_to_all | solution.py:279
  57.7 5.7 %all-to-all-start.3 = ((bf16[16,24,128]{2,1,0:T(8,128)(2,1)}), bf16[16,24,128]{2,1,0:T(8,128)(2,1)S(1)}, u32[]{:S(2)}, u32[]{:S(2)}) async-start(bf16[16,24,128]{2,1,0:T(8,128)(2,1)} %wave_sum.1), calls=%async_computation.3 | async-start | bytes 196608 | tf_op jit(solution)/shard_map/all_to_all | solution.py:289
  63.4 0.0 copy-done.1
  63.4 0.0 copy-done.10
  63.4 0.0 copy-done.11
  63.4 0.0 copy-done.14
  63.4 0.0 copy-done.15
  63.4 0.0 copy-start.3
  63.4 1.6 %copy-done.3 = bf16[32,2,16,1024]{3,2,1,0:T(8,128)(2,1)S(1)} copy-done((bf16[32,2,16,1024]{3,2,1,0:T(8,128)(2,1)S(1)}, bf16[32,2,16,1024]{3,2,1,0:T(8,128)(2,1)}, u32[]{:S(2)}) %copy-start.3) | copy-done | bytes 2097176
  65.0 0.0 copy-start.9
  65.0 0.0 copy-start.7
  65.0 5.3 %visibilities.1 = (f32[2,1,4096]{2,1,0:T(1,128)}, bf16[32,16,128]{2,1,0:T(8,128)(2,1)}) custom-call(bf16[32,16,128]{2,1,0:T(8,128)(2,1)S(1)} %all-to-all-done.got_ref, s32[1,4096]{1,0:T(1,128)S(1)} %copy-done.14, f32[1,4096]{1,0:T(1,128)S(1)} %copy-done.15, f32[2,1,4096]{2,1,0:T(1,128)S(1)} %copy-done.10, f32[2,1,4096]{2,1,0:T(1,128)S(1)} %copy-done.11, ...), custom_call_target="tpu_custom_call" | custom-call | tf_op jit(solution)/shard_map/visibilities/pallas_call | solution.py:253
  70.4 0.0 all-to-all-done.3.total_ref
  70.4 4.0 %all-to-all-start.1 = ((bf16[32,16,128]{2,1,0:T(8,128)(2,1)}), bf16[32,16,128]{2,1,0:T(8,128)(2,1)S(1)}, u32[]{:S(2)}, u32[]{:S(2)}) async-start(bf16[32,16,128]{2,1,0:T(8,128)(2,1)} %get-tuple-element.7), calls=%async_computation.1 | async-start | bytes 262144 | tf_op jit(solution)/shard_map/all_to_all | solution.py:299
  74.4 0.0 copy-done.9
  74.4 0.6 wave_back.1.wave_ref
  75.1 12.1 %all-to-all-done.1.got_ref = bf16[32,16,128]{2,1,0:T(8,128)(2,1)S(1)} async-done(((bf16[32,16,128]{2,1,0:T(8,128)(2,1)}), bf16[32,16,128]{2,1,0:T(8,128)(2,1)S(1)}, u32[]{:S(2)}, u32[]{:S(2)}) %all-to-all-start.1) | async-done | bytes 131104 | tf_op jit(solution)/shard_map/all_to_all | solution.py:299
  87.1 0.0 copy-done.7
  87.1 0.0 copy-start.4
  87.1 1.6 %copy-done.4 = bf16[32,2,16,1024]{3,2,1,0:T(8,128)(2,1)S(1)} copy-done((bf16[32,2,16,1024]{3,2,1,0:T(8,128)(2,1)S(1)}, bf16[32,2,16,1024]{3,2,1,0:T(8,128)(2,1)}, u32[]{:S(2)}) %copy-start.4) | copy-done | bytes 2097176
  88.7 1.5 %image_out.1 = f32[1,32,1024]{2,1,0:T(8,128)} custom-call(bf16[32,16,128]{2,1,0:T(8,128)(2,1)S(1)} %all-to-all-done.1.got_ref, f32[1,32,1024]{2,1,0:T(8,128)S(1)} %copy-done.7, f32[32,1024]{1,0:T(8,128)S(1)} %wave_back.1.wave_ref, bf16[32,2,16,1024]{3,2,1,0:T(8,128)(2,1)S(1)} %copy-done.1, bf16[32,2,16,1024]{3,2,1,0:T(8,128)(2,1)S(1)} %copy-done.4), custom_call_target="tpu_custom_call" | custom-call | tf_op jit(solution)/shard_map/image_out/pallas_call | solution.py:253
  (2 shorter events, 0.0 us)
Async XLA Ops:
  2.1 13.1 %collective-permute-start = (f32[8,1024]{1,0:T(8,128)S(1)}, f32[8,1024]{1,0:T(8,128)S(1)}, u32[]{:S(2)}, u32[]{:S(2)}) collective-permute-start(f32[8,1024]{1,0:T(8,128)S(1)} %concatenate.6), channel_id=1, source_target_pairs={{0,1},{1,2},{2,3},{3,4},{4,5},{5,6},{6,7},{7,8},{8,9},{9,10},{10,1... | collective-permute-start | bytes 98312 | tf_op jit(solution)/shard_map/ppermute | solution.py:276
  8.2 9.3 %collective-permute-start.1 = (f32[8,1024]{1,0:T(8,128)S(1)}, f32[8,1024]{1,0:T(8,128)S(1)}, u32[]{:S(2)}, u32[]{:S(2)}) collective-permute-start(f32[8,1024]{1,0:T(8,128)S(1)} %concatenate.7), channel_id=1, source_target_pairs={{1,0},{2,1},{3,2},{4,3},{5,4},{6,5},{7,6},{8,7},{9,8},{10,9},{11,1... | collective-permute-start | bytes 98312 | tf_op jit(solution)/shard_map/ppermute | solution.py:277
  17.5 0.9 %copy-start.5 = (f32[1,32,1024]{2,1,0:T(8,128)S(1)}, f32[1,32,1024]{2,1,0:T(8,128)}, u32[]{:S(2)}) copy-start(f32[1,32,1024]{2,1,0:T(8,128)} %image_ref.5) | copy-start | bytes 393220
  18.4 0.8 copy-start.8
  19.2 0.7 copy-start.12
  20.0 0.7 copy-start.13
  22.1 11.4 %all-to-all-start.2 = ((bf16[16,24,128]{2,1,0:T(8,128)(2,1)}), bf16[16,24,128]{2,1,0:T(8,128)(2,1)S(1)}, u32[]{:S(2)}, u32[]{:S(2)}) async-start(bf16[16,24,128]{2,1,0:T(8,128)(2,1)} %get-tuple-element.9), calls=%async_computation.2 | async-start | bytes 196608 | tf_op jit(solution)/shard_map/all_to_all | solution.py:287
  27.7 1.6 %copy-start = (bf16[32,2,16,1024]{3,2,1,0:T(8,128)(2,1)S(1)}, bf16[32,2,16,1024]{3,2,1,0:T(8,128)(2,1)}, u32[]{:S(2)}) copy-start(bf16[32,2,16,1024]{3,2,1,0:T(8,128)(2,1)} %constant.12.clone.cos_ref) | copy-start | bytes 6291460
  29.3 1.6 %copy-start.2 = (bf16[32,2,16,1024]{3,2,1,0:T(8,128)(2,1)S(1)}, bf16[32,2,16,1024]{3,2,1,0:T(8,128)(2,1)}, u32[]{:S(2)}) copy-start(bf16[32,2,16,1024]{3,2,1,0:T(8,128)(2,1)} %constant.13.clone.sin_ref) | copy-start | bytes 6291460
  30.9 0.9 %copy-start.6 = (f32[1,32,1024]{2,1,0:T(8,128)S(1)}, f32[1,32,1024]{2,1,0:T(8,128)}, u32[]{:S(2)}) copy-start(f32[1,32,1024]{2,1,0:T(8,128)} %image_ref.5) | copy-start | bytes 393220
  31.8 31.6 %copy-start.1 = (bf16[32,2,16,1024]{3,2,1,0:T(8,128)(2,1)S(1)}, bf16[32,2,16,1024]{3,2,1,0:T(8,128)(2,1)}, u32[]{:S(2)}) copy-start(bf16[32,2,16,1024]{3,2,1,0:T(8,128)(2,1)} %constant.12.clone.cos_ref) | copy-start | bytes 6291460
  31.8 31.6 %copy-start.10 = (f32[2,1,4096]{2,1,0:T(1,128)S(1)}, f32[2,1,4096]{2,1,0:T(1,128)}, u32[]{:S(2)}) copy-start(f32[2,1,4096]{2,1,0:T(1,128)} %seen_ref.1) | copy-start | bytes 98308
  31.8 31.6 %copy-start.11 = (f32[2,1,4096]{2,1,0:T(1,128)S(1)}, f32[2,1,4096]{2,1,0:T(1,128)}, u32[]{:S(2)}) copy-start(f32[2,1,4096]{2,1,0:T(1,128)} %dual_ref.1) | copy-start | bytes 98308
  31.8 31.6 %copy-start.14 = (s32[1,4096]{1,0:T(1,128)S(1)}, s32[1,4096]{1,0:T(1,128)}, u32[]{:S(2)}) copy-start(s32[1,4096]{1,0:T(1,128)} %cells_ref.1) | copy-start | bytes 49156
  31.8 31.6 %copy-start.15 = (f32[1,4096]{1,0:T(1,128)S(1)}, f32[1,4096]{1,0:T(1,128)}, u32[]{:S(2)}) copy-start(f32[1,4096]{1,0:T(1,128)} %gains_ref.1) | copy-start | bytes 49156
  33.5 24.2 %all-to-all-start = ((bf16[32,16,128]{2,1,0:T(8,128)(2,1)}), bf16[32,16,128]{2,1,0:T(8,128)(2,1)S(1)}, u32[]{:S(2)}, u32[]{:S(2)}) async-start(bf16[32,16,128]{2,1,0:T(8,128)(2,1)} %rows_out.1), calls=%async_computation | async-start | bytes 262144 | tf_op jit(solution)/shard_map/all_to_all | solution.py:279
  57.7 12.7 %all-to-all-start.3 = ((bf16[16,24,128]{2,1,0:T(8,128)(2,1)}), bf16[16,24,128]{2,1,0:T(8,128)(2,1)S(1)}, u32[]{:S(2)}, u32[]{:S(2)}) async-start(bf16[16,24,128]{2,1,0:T(8,128)(2,1)} %wave_sum.1), calls=%async_computation.3 | async-start | bytes 196608 | tf_op jit(solution)/shard_map/all_to_all | solution.py:289
  63.4 1.6 %copy-start.3 = (bf16[32,2,16,1024]{3,2,1,0:T(8,128)(2,1)S(1)}, bf16[32,2,16,1024]{3,2,1,0:T(8,128)(2,1)}, u32[]{:S(2)}) copy-start(bf16[32,2,16,1024]{3,2,1,0:T(8,128)(2,1)} %constant.13.clone.sin_ref) | copy-start | bytes 6291460
  65.0 9.4 %copy-start.9 = (f32[16,1024]{1,0:T(8,128)S(1)}, f32[16,1024]{1,0:T(8,128)}, u32[]{:S(2)}) copy-start(f32[16,1024]{1,0:T(8,128)} %constant.15.clone.weights_ref) | copy-start | bytes 196612
  65.0 22.1 %copy-start.7 = (f32[1,32,1024]{2,1,0:T(8,128)S(1)}, f32[1,32,1024]{2,1,0:T(8,128)}, u32[]{:S(2)}) copy-start(f32[1,32,1024]{2,1,0:T(8,128)} %image_ref.5) | copy-start | bytes 393220
  70.4 16.8 %all-to-all-start.1 = ((bf16[32,16,128]{2,1,0:T(8,128)(2,1)}), bf16[32,16,128]{2,1,0:T(8,128)(2,1)S(1)}, u32[]{:S(2)}, u32[]{:S(2)}) async-start(bf16[32,16,128]{2,1,0:T(8,128)(2,1)} %get-tuple-element.7), calls=%async_computation.1 | async-start | bytes 262144 | tf_op jit(solution)/shard_map/all_to_all | solution.py:299
  87.1 1.6 %copy-start.4 = (bf16[32,2,16,1024]{3,2,1,0:T(8,128)(2,1)S(1)}, bf16[32,2,16,1024]{3,2,1,0:T(8,128)(2,1)}, u32[]{:S(2)}) copy-start(bf16[32,2,16,1024]{3,2,1,0:T(8,128)(2,1)} %constant.13.clone.sin_ref) | copy-start | bytes 6291460

commit v2 on v1

v2 whole, which is shorter than its diff:
```python
import math

import jax
import jax.numpy as jnp
import numpy as np
from jax import lax
from jax.experimental import pallas as pl
from jax.experimental.pallas import tpu as pltpu
from jax.sharding import PartitionSpec as P

N = 1024
HALF = 512
ROWS = 32
FACETS = 32
CHANNELS = 16
VIS = 4096
STEP = 512

low_taps = (
    -0.010597401784997278,
    0.032883011666982945,
    0.030841381835986965,
    -0.18703481171888114,
    -0.02798376941698385,
    0.6308807679295904,
    0.7148465705525415,
    0.23037781330885523,
)
high_taps = (
    -0.23037781330885523,
    0.7148465705525415,
    -0.6308807679295904,
    -0.02798376941698385,
    0.18703481171888114,
    0.030841381835986965,
    -0.032883011666982945,
    -0.010597401784997278,
)
tau_step = 0.5
bound_level = 3.0
f32 = jnp.float32
bf16 = jnp.bfloat16


def fourier_tables():
    index = np.arange(HALF, dtype=np.int32)
    product = index[:, None] * index[None, :] % N
    angle = product.astype(np.float32) * np.float32(2.0 * math.pi / N)
    scale = np.float32(1.0 / math.sqrt(N))
    shape = (FACETS // 2, 2, 16, HALF)
    return (
        (np.cos(angle) * scale).astype(bf16).reshape(shape),
        (np.sin(angle) * scale).astype(bf16).reshape(shape),
    )


def tap_pair(shift):
    even = low_taps[shift + 3] if 0 <= shift + 3 < 8 else 0.0
    odd = high_taps[shift + 4] if 0 <= shift + 4 < 8 else 0.0
    return even, odd


def row_weights(above, own, below):
    place = lax.broadcasted_iota(jnp.int32, (48, 48), 0)
    position = place - 4
    line = lax.broadcasted_iota(jnp.int32, (48, 48), 1) - 8
    even = position % 2 == 0
    taps = jnp.zeros((48, 48), f32)
    for shift in range(-4, 5):
        pair = tap_pair(shift)
        taps = jnp.where(line - position == shift, jnp.where(even, *pair), taps)
    inside = jnp.maximum(jnp.maximum(-line, line - ROWS + 1), 0)
    distance = jnp.where(
        place < 4,
        jnp.maximum(line + 1, 0),
        jnp.where(place < 36, inside, jnp.maximum(ROWS - line, 0)),
    )
    width = jnp.where(place < 4, above, jnp.where(place < 36, own, below))
    return jnp.where((distance.astype(f32) <= width) & (place < 40), taps, 0.0)


def exchange_groups(groups):
    lane = lax.broadcasted_iota(jnp.int32, groups[0].shape, 1)
    g = list(groups)
    for width, pairs in ((64, ((0, 2), (1, 3))), (32, ((0, 1), (2, 3)))):
        first = (lane % (2 * width)) < width
        for a, b in pairs:
            x, y = g[a], g[b]
            g[a] = jnp.where(first, x, pltpu.roll(y, width, 1))
            g[b] = jnp.where(first, pltpu.roll(x, 128 - width, 1), y)
    return g


def pack(real, imag, out_ref):
    for block in range(8):
        span = slice(128 * block, 128 * (block + 1))
        groups = [real[:16, span], real[16:, span], imag[:16, span], imag[16:, span]]
        for d, chunk in enumerate(exchange_groups(groups)):
            out_ref[4 * block + d] = chunk.astype(bf16)


def dot(a, b):
    return jnp.dot(a, b, preferred_element_type=f32)


def signs(dims):
    return jnp.where(lax.broadcasted_iota(jnp.int32, dims, 1) % 2 == 0, 1.0, -1.0)


def quarters(low, high):
    sign = signs(low.shape).astype(bf16)
    return jnp.concatenate([low, high, low * sign, high * sign], axis=0)


def whole(products):
    rows = products.shape[0] // 4
    sign = signs((rows, HALF))
    part = [products[rows * t : rows * t + rows] for t in range(4)]
    return jnp.concatenate([part[0] + sign * part[1], part[2] + sign * part[3]], axis=1)


def regrouped(table_ref):
    return jnp.concatenate([table_ref[:, h].reshape(256, HALF) for h in range(2)], axis=0)


def split(pieces):
    return (
        jnp.concatenate([p[:, :256] for p in pieces], axis=1),
        jnp.concatenate([p[:, 256:] for p in pieces], axis=1),
    )


def forward_kernel(
    margin_ref, image_ref, cos_ref, sin_ref,
    out_ref, low_ref, high_ref, held_ref, cos_out, sin_out, image_sem, table_sems,
):
    image_copy = pltpu.make_async_copy(image_ref.at[0], held_ref, image_sem)
    image_copy.start()
    copies = [
        pltpu.make_async_copy(cos_ref, cos_out, table_sems.at[0]),
        pltpu.make_async_copy(sin_ref, sin_out, table_sems.at[1]),
    ]
    for copy in copies:
        copy.start()
    image_copy.wait()
    width = jnp.broadcast_to(margin_ref[0].astype(f32), (8, N))
    line = lax.broadcasted_iota(jnp.int32, (8, N), 0)
    low_ref[...] = jnp.where(line == 0, width, held_ref[24:, :])
    high_ref[...] = jnp.where(line == 7, width, held_ref[:8, :])
    flat = held_ref[...].astype(bf16)
    left = quarters(flat[:, :HALF], flat[:, HALF:])
    copies[0].wait()
    real = whole(dot(left, cos_out[...].reshape(HALF, HALF)))
    copies[1].wait()
    imag = -whole(dot(left, sin_out[...].reshape(HALF, HALF)))
    pack(real, imag, out_ref)


def vis_kernel(
    got_ref, cells_ref, gains_ref, seen_ref, dual_ref, cos_ref, sin_ref, dual_out, out_ref
):
    turned = got_ref[...].reshape(512, 128).T
    left = quarters(
        *split(
            [
                jnp.concatenate(
                    [turned[32 * h : 32 * h + 32], turned[64 + 32 * h : 96 + 32 * h]], axis=0
                )
                for h in range(2)
            ]
        )
    )
    by_cos = whole(dot(left, regrouped(cos_ref)))
    by_sin = whole(dot(left, regrouped(sin_ref)))
    grid = (by_cos[:32] + by_sin[32:], by_cos[32:] - by_sin[:32])
    stacked = jnp.concatenate(
        [part[:, 256 * t : 256 * t + 256] for part in grid for t in range(4)], axis=0
    )
    upper = stacked.astype(bf16)
    lower = (stacked - upper.astype(f32)).astype(bf16)
    lines = jnp.concatenate([upper, lower], axis=1)
    cell_lane = lax.broadcasted_iota(jnp.int32, (256, STEP), 0)
    cell_line = lax.broadcasted_iota(jnp.int32, (128, STEP), 0)
    hold = jnp.zeros((256, 256), f32)
    for step in range(VIS // STEP):
        span = slice(STEP * step, STEP * (step + 1))
        cell = cells_ref[:, span]
        lane = cell & 255
        line = ((cell >> 8) & 3) * 32 + (cell >> 10)
        gains = gains_ref[:, span]
        here = jnp.where(cell_lane == lane, 1.0, 0.0).astype(bf16)
        chosen = cell_line == line
        values = dot(lines, jnp.concatenate([here, here], axis=0))
        spread = []
        for c in range(2):
            picked = jnp.sum(
                jnp.where(chosen, values[128 * c : 128 * c + 128], 0.0), axis=0, keepdims=True
            )
            fresh = (dual_ref[c, :, span] + (gains * picked - seen_ref[c, :, span])) / 2.0
            dual_out[c, :, span] = fresh
            spread.append(jnp.where(chosen, gains * fresh, 0.0).astype(bf16))
        hold = hold + lax.dot_general(
            jnp.concatenate(spread, axis=0),
            here,
            (((1,), (1,)), ((), ())),
            preferred_element_type=f32,
        )
    held = hold.astype(bf16)
    held = jnp.concatenate(
        [
            jnp.concatenate(
                [held[128 * c + 32 * t : 128 * c + 32 * t + 32] for t in range(4)], axis=1
            )
            for c in range(2)
        ],
        axis=0,
    )
    left = quarters(held[:, :HALF], held[:, HALF:])
    by_cos = whole(dot(left, cos_ref[...].reshape(HALF, HALF)))
    by_sin = whole(dot(left, sin_ref[...].reshape(HALF, HALF)))
    pack(by_cos[:32] - by_sin[32:], by_sin[:32] + by_cos[32:], out_ref)


def filtered_columns(values, adjoint):
    rows = values.shape[0]
    padded = jnp.concatenate([values, jnp.zeros((rows, 128), f32)], axis=1)
    even = lax.broadcasted_iota(jnp.int32, (rows, N), 1) % 2 == 0
    total = jnp.zeros((rows, N), f32)
    for shift in range(-4, 5):
        moved = pltpu.roll(padded, (-shift) % (N + 128), 1)[:, :N] if shift else values
        pair = tap_pair(-shift if adjoint else shift)
        if adjoint and shift % 2:
            pair = pair[::-1]
        total = total + moved * jnp.where(even, *pair)
    return total


def exact_dot(a, b, dims):
    return lax.dot_general(
        a, b, (dims, ((), ())), precision=lax.Precision.HIGHEST, preferred_element_type=f32
    )


def wave_kernel(
    margin_ref, image_ref, low_ref, high_ref, coef_ref, square_ref, rows_ref
):
    above = jnp.broadcast_to(low_ref[0:1, 0:48], (48, 48))
    below = jnp.broadcast_to(high_ref[7:8, 0:48], (48, 48))
    rows = row_weights(above, margin_ref[0].astype(f32), below)
    rows_ref[...] = rows
    extended = jnp.concatenate([low_ref[...], image_ref[...], high_ref[...]], axis=0)
    coef = filtered_columns(exact_dot(rows, extended, ((1,), (0,))), False)
    coef_ref[...] = coef
    square_ref[...] = (coef * coef)[:40].astype(bf16)


def back_kernel(coef_ref, rows_ref, *refs):
    total = sum(ref[...].astype(f32) for ref in refs[:-1])
    factor = bound_level / jnp.maximum(jnp.sqrt(total), bound_level)
    mixed = exact_dot(rows_ref[0:40, :], coef_ref[0:40, :] * factor, ((0,), (0,)))
    refs[-1][...] = filtered_columns(mixed[8:40], True)


def join_kernel(*refs):
    refs[-1][...] = sum(ref[...].astype(f32) for ref in refs[:-1]).astype(bf16)


def final_kernel(got_ref, image_ref, wave_ref, cos_ref, sin_ref, out_ref):
    turned = got_ref[...].reshape(512, 128).T
    real = quarters(*split([turned[:32], turned[32:64]]))
    imag = quarters(*split([turned[64:96], turned[96:]]))
    data = whole(dot(real, regrouped(cos_ref)) - dot(imag, regrouped(sin_ref)))
    total = data + wave_ref[...]
    out_ref[0] = jnp.maximum(image_ref[...] - tau_step * total, 0.0)


in_vmem = pl.BlockSpec(memory_space=pltpu.VMEM)
in_smem = pl.BlockSpec(memory_space=pltpu.SMEM)
in_hbm = pl.BlockSpec(memory_space=pltpu.HBM)


def call(kernel, name, out_shape, *args, specs=None, scratch=(), room=12):
    return pl.pallas_call(
        kernel,
        out_shape=out_shape,
        in_specs=specs or [in_vmem] * len(args),
        out_specs=jax.tree.map(lambda _: in_vmem, out_shape),
        scratch_shapes=list(scratch),
        compiler_params=pltpu.CompilerParams(vmem_limit_bytes=room * 1024 * 1024),
        name=name,
    )(*args)


def shape(dims, kind):
    return jax.ShapeDtypeStruct(dims, kind)


def swapped(value, steps):
    moved = [lax.ppermute(value, "chan", [(i, i ^ s) for i in range(CHANNELS)]) for s in steps]
    return [value] + moved


def local(image, margin, cells, weights, observed, dual_start):
    cos_table, sin_table = (jnp.asarray(t) for t in fourier_tables())
    chunks = shape((FACETS, 16, 128), bf16)
    squares = shape((40, N), bf16)
    edge = shape((8, N), f32)
    table = shape(cos_table.shape, bf16)
    up = [(i, i + 1) for i in range(FACETS - 1)]
    down = [(i + 1, i) for i in range(FACETS - 1)]
    sent, low, high, held, cos_held, sin_held = call(
        forward_kernel,
        "rows_out",
        (chunks, edge, edge, shape((ROWS, N), f32), table, table),
        margin, image, cos_table, sin_table,
        specs=[in_smem] + [in_hbm] * 3,
        scratch=[pltpu.SemaphoreType.DMA, pltpu.SemaphoreType.DMA((2,))],
    )
    got = lax.all_to_all(sent, "slab", 0, 0, tiled=True)
    low = lax.ppermute(low, "slab", up)
    high = lax.ppermute(high, "slab", down)
    coef, square, rows = call(
        wave_kernel,
        "wave_out",
        (shape((48, N), f32), squares, shape((48, 48), f32)),
        margin, held, low, high,
        specs=[in_smem] + [in_vmem] * 3,
    )
    part = call(join_kernel, "wave_part", squares, *swapped(square, (1, 8, 9)))
    got, part = lax.optimization_barrier((got, part))
    dual, back = call(
        vis_kernel,
        "visibilities",
        (shape((2, 1, VIS), f32), chunks),
        got, cells, weights, observed, dual_start, cos_held, sin_held,
    )
    returned = lax.all_to_all(back, "slab", 0, 0, tiled=True)
    wave = call(
        back_kernel, "wave_back", shape((ROWS, N), f32), coef, rows, *swapped(part, (2, 4, 6))
    )
    fresh = call(
        final_kernel, "image_out", shape((1, ROWS, N), f32),
        returned, held, wave, cos_held, sin_held,
    )
    return (fresh, dual)


def solution(mesh):
    in_specs = (
        P("chan", "slab", None),
        P("slab"),
        P("chan", "slab"),
        P("chan", "slab"),
        P(None, "chan", "slab"),
        P(None, "chan", "slab"),
    )
    out_specs = (P("chan", "slab", None), P(None, "chan", "slab"))
    return jax.shard_map(local, mesh=mesh, in_specs=in_specs, out_specs=out_specs, check_vma=False)
```

time: 91.1 us -> 80 us (0.88)
  the two profiles are of different devices: /device:TPU:10 before, /device:TPU:8 now
where the time goes in v2:
time: 80 us; the launch traced here: 79.3 us
  starting transfers between devices  54.4 us (68%)
  waiting for transfers between devices  12 us (15%)
  Pallas kernels  8.48 us (11%)
  local copies, waits for them, and re-layouts  3.01 us (4%)
  between operations  1.49 us (2%)
    ppermute x6, starting transfers between devices, swapped(): lax.ppermute(value, 'chan', [(i, i ^ s) for i in range(CHANNELS)])  18.1 us
    all_to_all x1, starting transfers between devices, local(): got = lax.all_to_all(sent, 'slab', 0, 0, tiled=True)  16.2 us
    all_to_all x1, starting transfers between devices, local(): returned = lax.all_to_all(back, 'slab', 0, 0, tiled=True)  11.2 us
    ppermute x6, waiting for transfers between devices, swapped(): lax.ppermute(value, 'chan', [(i, i ^ s) for i in range(CHANNELS)])  9.09 us
    pallas_call x6, Pallas kernels, call(): pl.pallas_call(kernel, out_shape=out_shape, in_specs=specs or [in_vmem] *...  8.48 us
    ppermute x1, starting transfers between devices, local(): high = lax.ppermute(high, 'slab', down)  4.58 us
    ppermute x1, starting transfers between devices, local(): low = lax.ppermute(low, 'slab', up)  4.27 us
    unnamed x14, local copies, waits for them, and re-layouts  3.01 us
  transfers between devices with their start and end apart: 10, of which 6 were waited for; matrix products, arithmetic and copies ran while one was open for 0% of the time, Pallas kernels for 2%

profile of v2, /device:TPU:8, one launch (start us, length us, event | category | flops | bytes accessed | tf_op | source)
XLA Modules:
  0.0 79.3 jit_solution(12530326157530124183)
XLA Ops:
  1.3 0.0 copy-start
  1.3 1.0 %copy-done = bf16[16,2,16,512]{3,2,1,0:T(8,128)(2,1)S(1)} copy-done((bf16[16,2,16,512]{3,2,1,0:T(8,128)(2,1)S(1)}, bf16[16,2,16,512]{3,2,1,0:T(8,128)(2,1)}, u32[]{:S(2)}) %copy-start) | copy-done | bytes 524312
  2.3 0.0 copy-start.1
  2.3 1.0 %copy-done.1 = bf16[16,2,16,512]{3,2,1,0:T(8,128)(2,1)S(1)} copy-done((bf16[16,2,16,512]{3,2,1,0:T(8,128)(2,1)S(1)}, bf16[16,2,16,512]{3,2,1,0:T(8,128)(2,1)}, u32[]{:S(2)}) %copy-start.1) | copy-done | bytes 524312
  3.4 0.0 copy-start.2
  3.4 0.9 %copy-done.2 = f32[1,32,1024]{2,1,0:T(8,128)S(1)} copy-done((f32[1,32,1024]{2,1,0:T(8,128)S(1)}, f32[1,32,1024]{2,1,0:T(8,128)}, u32[]{:S(2)}) %copy-start.2) | copy-done | bytes 131096
  4.3 1.5 %rows_out.1 = (bf16[32,16,128]{2,1,0:T(8,128)(2,1)}, f32[8,1024]{1,0:T(8,128)S(1)}, f32[8,1024]{1,0:T(8,128)S(1)}, f32[32,1024]{1,0:T(8,128)S(1)}, bf16[16,2,16,...) custom-call(s32[1]{0:T(128)S(6)} %copy.10.margin_ref, f32[1,32,1024]{2,1,0:T(8,128)S(1)} %copy-done.2, ...), custom_call_target="tpu_custom_call" | custom-call | tf_op jit(solution)/shard_map/rows_out/pallas_call | solution.py:283
  5.8 16.2 %all-to-all-start = ((bf16[32,16,128]{2,1,0:T(8,128)(2,1)}), bf16[32,16,128]{2,1,0:T(8,128)(2,1)S(1)}, u32[]{:S(2)}, u32[]{:S(2)}) async-start(bf16[32,16,128]{2,1,0:T(8,128)(2,1)} %get-tuple-element.15), calls=%async_computation | async-start | bytes 262144 | tf_op jit(solution)/shard_map/all_to_all | solution.py:319
  22.0 4.3 %collective-permute-start = (f32[8,1024]{1,0:T(8,128)S(1)}, f32[8,1024]{1,0:T(8,128)S(1)}, u32[]{:S(2)}, u32[]{:S(2)}) collective-permute-start(f32[8,1024]{1,0:T(8,128)S(1)} %get-tuple-element.17), channel_id=1, source_target_pairs={{0,1},{1,2},{2,3},{3,4},{4,5},{5,6},{6,7},{7,8},{8,9},{9,10},{10,1... | collective-permute-start | bytes 98312 | tf_op jit(solution)/shard_map/ppermute | solution.py:320
  26.3 4.6 %collective-permute-start.1 = (f32[8,1024]{1,0:T(8,128)S(1)}, f32[8,1024]{1,0:T(8,128)S(1)}, u32[]{:S(2)}, u32[]{:S(2)}) collective-permute-start(f32[8,1024]{1,0:T(8,128)S(1)} %get-tuple-element.18), channel_id=1, source_target_pairs={{1,0},{2,1},{3,2},{4,3},{5,4},{6,5},{7,6},{8,7},{9,8},{10,9},{11,1... | collective-permute-start | bytes 98312 | tf_op jit(solution)/shard_map/ppermute | solution.py:321
  30.9 0.6 collective-permute-done.low_ref
  31.5 2.3 %collective-permute-done.1.high_ref = f32[8,1024]{1,0:T(8,128)S(1)} collective-permute-done((f32[8,1024]{1,0:T(8,128)S(1)}, f32[8,1024]{1,0:T(8,128)S(1)}, u32[]{:S(2)}, u32[]{:S(2)}) %collective-permute-start.1) | collective-permute-done | bytes 32800 | tf_op jit(solution)/shard_map/ppermute | solution.py:321
  33.7 0.7 wave_out.1
  34.5 0.0 copy-start.3
  34.5 0.0 copy-start.4
  34.5 0.0 copy-start.5
  34.5 0.0 copy-start.6
  34.5 2.1 %collective-permute-start.2 = (bf16[40,1024]{1,0:T(8,128)(2,1)S(1)}, bf16[40,1024]{1,0:T(8,128)(2,1)S(1)}, u32[]{:S(2)}, u32[]{:S(2)}) collective-permute-start(bf16[40,1024]{1,0:T(8,128)(2,1)S(1)} %get-tuple-element.19.refs_0_), channel_id=1, source_target_pairs={{0,32},{32,0},{64,96},{96,64},{128,160},{160,128},{192,224},{224,1... | collective-permute-start | bytes 245768 | tf_op jit(solution)/shard_map/ppermute | solution.py:299
  36.6 3.3 %collective-permute-start.3 = (bf16[40,1024]{1,0:T(8,128)(2,1)S(1)}, bf16[40,1024]{1,0:T(8,128)(2,1)S(1)}, u32[]{:S(2)}, u32[]{:S(2)}) collective-permute-start(bf16[40,1024]{1,0:T(8,128)(2,1)S(1)} %get-tuple-element.19.refs_0_), channel_id=1, source_target_pairs={{0,256},{32,288},{64,320},{96,352},{128,384},{160,416},{192,448},{... | collective-permute-start | bytes 245768 | tf_op jit(solution)/shard_map/ppermute | solution.py:299
  39.9 2.4 %collective-permute-start.4 = (bf16[40,1024]{1,0:T(8,128)(2,1)S(1)}, bf16[40,1024]{1,0:T(8,128)(2,1)S(1)}, u32[]{:S(2)}, u32[]{:S(2)}) collective-permute-start(bf16[40,1024]{1,0:T(8,128)(2,1)S(1)} %get-tuple-element.19.refs_0_), channel_id=1, source_target_pairs={{0,288},{32,256},{64,352},{96,320},{128,416},{160,384},{192,480},{... | collective-permute-start | bytes 245768 | tf_op jit(solution)/shard_map/ppermute | solution.py:299
  42.3 0.0 collective-permute-done.2.refs_1_
  42.3 1.0 %collective-permute-done.3.refs_2_ = bf16[40,1024]{1,0:T(8,128)(2,1)S(1)} collective-permute-done((bf16[40,1024]{1,0:T(8,128)(2,1)S(1)}, bf16[40,1024]{1,0:T(8,128)(2,1)S(1)}, u32[]{:S(2)}, u32[]{:S(2)}) %collective-permute-start.3) | collective-permute-done | bytes 81952 | tf_op jit(solution)/shard_map/ppermute | solution.py:299
  43.3 2.9 %collective-permute-done.4.refs_3_ = bf16[40,1024]{1,0:T(8,128)(2,1)S(1)} collective-permute-done((bf16[40,1024]{1,0:T(8,128)(2,1)S(1)}, bf16[40,1024]{1,0:T(8,128)(2,1)S(1)}, u32[]{:S(2)}, u32[]{:S(2)}) %collective-permute-start.4) | collective-permute-done | bytes 81952 | tf_op jit(solution)/shard_map/ppermute | solution.py:299
  46.3 0.0 all-to-all-done.got_ref
  46.3 0.0 copy-done.3
  46.3 0.0 copy-done.4
  46.3 0.0 copy-done.5
  46.3 0.0 copy-done.6
  46.3 4.5 %visibilities.1 = (f32[2,1,4096]{2,1,0:T(1,128)}, bf16[32,16,128]{2,1,0:T(8,128)(2,1)}) custom-call(bf16[32,16,128]{2,1,0:T(8,128)(2,1)S(1)} %all-to-all-done.got_ref, s32[1,4096]{1,0:T(1,128)S(1)} %copy-done.5, f32[1,4096]{1,0:T(1,128)S(1)} %copy-done.6, f32[2,1,4096]{2,1,0:T(1,128)S(1)} %copy-done.3, f32[2,1,4096]{2,1,0:T(1,128)S(1)} %copy-done.4, ...), custom_call_target="tpu_custom_call" | custom-call | tf_op jit(solution)/shard_map/visibilities/pallas_call | solution.py:283
  50.8 11.2 %all-to-all-start.1 = ((bf16[32,16,128]{2,1,0:T(8,128)(2,1)}), bf16[32,16,128]{2,1,0:T(8,128)(2,1)S(1)}, u32[]{:S(2)}, u32[]{:S(2)}) async-start(bf16[32,16,128]{2,1,0:T(8,128)(2,1)} %get-tuple-element.23), calls=%async_computation.1 | async-start | bytes 262144 | tf_op jit(solution)/shard_map/all_to_all | solution.py:337
  62.1 3.4 %collective-permute-start.5 = (bf16[40,1024]{1,0:T(8,128)(2,1)S(1)}, bf16[40,1024]{1,0:T(8,128)(2,1)S(1)}, u32[]{:S(2)}, u32[]{:S(2)}) collective-permute-start(bf16[40,1024]{1,0:T(8,128)(2,1)S(1)} %wave_part.1.refs_0_), channel_id=1, source_target_pairs={{0,64},{32,96},{64,0},{96,32},{128,192},{160,224},{192,128},{224,1... | collective-permute-start | bytes 245768 | tf_op jit(solution)/shard_map/ppermute | solution.py:299
  65.5 4.6 %collective-permute-start.6 = (bf16[40,1024]{1,0:T(8,128)(2,1)S(1)}, bf16[40,1024]{1,0:T(8,128)(2,1)S(1)}, u32[]{:S(2)}, u32[]{:S(2)}) collective-permute-start(bf16[40,1024]{1,0:T(8,128)(2,1)S(1)} %wave_part.1.refs_0_), channel_id=1, source_target_pairs={{0,128},{32,160},{64,192},{96,224},{128,0},{160,32},{192,64},{224,... | collective-permute-start | bytes 245768 | tf_op jit(solution)/shard_map/ppermute | solution.py:299
  70.1 2.4 %collective-permute-start.7 = (bf16[40,1024]{1,0:T(8,128)(2,1)S(1)}, bf16[40,1024]{1,0:T(8,128)(2,1)S(1)}, u32[]{:S(2)}, u32[]{:S(2)}) collective-permute-start(bf16[40,1024]{1,0:T(8,128)(2,1)S(1)} %wave_part.1.refs_0_), channel_id=1, source_target_pairs={{0,192},{32,224},{64,128},{96,160},{128,64},{160,96},{192,0},{224,... | collective-permute-start | bytes 245768 | tf_op jit(solution)/shard_map/ppermute | solution.py:299
  72.5 0.0 collective-permute-done.5.refs_1_
  72.5 0.8 collective-permute-done.6.refs_2_
  73.3 4.4 %collective-permute-done.7.refs_3_ = bf16[40,1024]{1,0:T(8,128)(2,1)S(1)} collective-permute-done((bf16[40,1024]{1,0:T(8,128)(2,1)S(1)}, bf16[40,1024]{1,0:T(8,128)(2,1)S(1)}, u32[]{:S(2)}, u32[]{:S(2)}) %collective-permute-start.7) | collective-permute-done | bytes 81952 | tf_op jit(solution)/shard_map/ppermute | solution.py:299
  77.7 0.6 wave_back.1.wave_ref
  78.3 0.0 all-to-all-done.1.got_ref
  78.3 1.0 %image_out.1 = f32[1,32,1024]{2,1,0:T(8,128)} custom-call(bf16[32,16,128]{2,1,0:T(8,128)(2,1)S(1)} %all-to-all-done.1.got_ref, f32[32,1024]{1,0:T(8,128)S(1)} %get-tuple-element.16.image_ref, f32[32,1024]{1,0:T(8,128)S(1)} %wave_back.1.wave_ref, bf16[16,2,16,512]{3,2,1,0:T(8,128)(2,1)S(1)} %get-tuple-element.21.cos_ref, ...), custom_call_target="tpu_custom_call" | custom-call | tf_op jit(solution)/shard_map/image_out/pallas_call | solution.py:283
  (1 shorter events, 0.0 us)
Async XLA Ops:
  1.3 1.0 %copy-start = (bf16[16,2,16,512]{3,2,1,0:T(8,128)(2,1)S(1)}, bf16[16,2,16,512]{3,2,1,0:T(8,128)(2,1)}, u32[]{:S(2)}) copy-start(bf16[16,2,16,512]{3,2,1,0:T(8,128)(2,1)} %constant.4.clone.cos_ref) | copy-start | bytes 1572868
  2.3 1.0 %copy-start.1 = (bf16[16,2,16,512]{3,2,1,0:T(8,128)(2,1)S(1)}, bf16[16,2,16,512]{3,2,1,0:T(8,128)(2,1)}, u32[]{:S(2)}) copy-start(bf16[16,2,16,512]{3,2,1,0:T(8,128)(2,1)} %constant.5.clone.sin_ref) | copy-start | bytes 1572868
  3.4 0.9 %copy-start.2 = (f32[1,32,1024]{2,1,0:T(8,128)S(1)}, f32[1,32,1024]{2,1,0:T(8,128)}, u32[]{:S(2)}) copy-start(f32[1,32,1024]{2,1,0:T(8,128)} %image_ref.1) | copy-start | bytes 393220
  5.8 40.4 %all-to-all-start = ((bf16[32,16,128]{2,1,0:T(8,128)(2,1)}), bf16[32,16,128]{2,1,0:T(8,128)(2,1)S(1)}, u32[]{:S(2)}, u32[]{:S(2)}) async-start(bf16[32,16,128]{2,1,0:T(8,128)(2,1)} %get-tuple-element.15), calls=%async_computation | async-start | bytes 262144 | tf_op jit(solution)/shard_map/all_to_all | solution.py:319
  22.0 9.5 %collective-permute-start = (f32[8,1024]{1,0:T(8,128)S(1)}, f32[8,1024]{1,0:T(8,128)S(1)}, u32[]{:S(2)}, u32[]{:S(2)}) collective-permute-start(f32[8,1024]{1,0:T(8,128)S(1)} %get-tuple-element.17), channel_id=1, source_target_pairs={{0,1},{1,2},{2,3},{3,4},{4,5},{5,6},{6,7},{7,8},{8,9},{9,10},{10,1... | collective-permute-start | bytes 98312 | tf_op jit(solution)/shard_map/ppermute | solution.py:320
  26.3 7.5 %collective-permute-start.1 = (f32[8,1024]{1,0:T(8,128)S(1)}, f32[8,1024]{1,0:T(8,128)S(1)}, u32[]{:S(2)}, u32[]{:S(2)}) collective-permute-start(f32[8,1024]{1,0:T(8,128)S(1)} %get-tuple-element.18), channel_id=1, source_target_pairs={{1,0},{2,1},{3,2},{4,3},{5,4},{6,5},{7,6},{8,7},{9,8},{10,9},{11,1... | collective-permute-start | bytes 98312 | tf_op jit(solution)/shard_map/ppermute | solution.py:321
  34.5 11.8 %copy-start.3 = (f32[2,1,4096]{2,1,0:T(1,128)S(1)}, f32[2,1,4096]{2,1,0:T(1,128)}, u32[]{:S(2)}) copy-start(f32[2,1,4096]{2,1,0:T(1,128)} %seen_ref.1) | copy-start | bytes 98308
  34.5 11.8 %copy-start.4 = (f32[2,1,4096]{2,1,0:T(1,128)S(1)}, f32[2,1,4096]{2,1,0:T(1,128)}, u32[]{:S(2)}) copy-start(f32[2,1,4096]{2,1,0:T(1,128)} %dual_ref.1) | copy-start | bytes 98308
  34.5 11.8 %copy-start.5 = (s32[1,4096]{1,0:T(1,128)S(1)}, s32[1,4096]{1,0:T(1,128)}, u32[]{:S(2)}) copy-start(s32[1,4096]{1,0:T(1,128)} %cells_ref.1) | copy-start | bytes 49156
  34.5 11.8 %copy-start.6 = (f32[1,4096]{1,0:T(1,128)S(1)}, f32[1,4096]{1,0:T(1,128)}, u32[]{:S(2)}) copy-start(f32[1,4096]{1,0:T(1,128)} %gains_ref.1) | copy-start | bytes 49156
  34.5 7.7 %collective-permute-start.2 = (bf16[40,1024]{1,0:T(8,128)(2,1)S(1)}, bf16[40,1024]{1,0:T(8,128)(2,1)S(1)}, u32[]{:S(2)}, u32[]{:S(2)}) collective-permute-start(bf16[40,1024]{1,0:T(8,128)(2,1)S(1)} %get-tuple-element.19.refs_0_), channel_id=1, source_target_pairs={{0,32},{32,0},{64,96},{96,64},{128,160},{160,128},{192,224},{224,1... | collective-permute-start | bytes 245768 | tf_op jit(solution)/shard_map/ppermute | solution.py:299
  36.6 6.7 %collective-permute-start.3 = (bf16[40,1024]{1,0:T(8,128)(2,1)S(1)}, bf16[40,1024]{1,0:T(8,128)(2,1)S(1)}, u32[]{:S(2)}, u32[]{:S(2)}) collective-permute-start(bf16[40,1024]{1,0:T(8,128)(2,1)S(1)} %get-tuple-element.19.refs_0_), channel_id=1, source_target_pairs={{0,256},{32,288},{64,320},{96,352},{128,384},{160,416},{192,448},{... | collective-permute-start | bytes 245768 | tf_op jit(solution)/shard_map/ppermute | solution.py:299
  39.9 6.3 %collective-permute-start.4 = (bf16[40,1024]{1,0:T(8,128)(2,1)S(1)}, bf16[40,1024]{1,0:T(8,128)(2,1)S(1)}, u32[]{:S(2)}, u32[]{:S(2)}) collective-permute-start(bf16[40,1024]{1,0:T(8,128)(2,1)S(1)} %get-tuple-element.19.refs_0_), channel_id=1, source_target_pairs={{0,288},{32,256},{64,352},{96,320},{128,416},{160,384},{192,480},{... | collective-permute-start | bytes 245768 | tf_op jit(solution)/shard_map/ppermute | solution.py:299
  50.8 27.5 %all-to-all-start.1 = ((bf16[32,16,128]{2,1,0:T(8,128)(2,1)}), bf16[32,16,128]{2,1,0:T(8,128)(2,1)S(1)}, u32[]{:S(2)}, u32[]{:S(2)}) async-start(bf16[32,16,128]{2,1,0:T(8,128)(2,1)} %get-tuple-element.23), calls=%async_computation.1 | async-start | bytes 262144 | tf_op jit(solution)/shard_map/all_to_all | solution.py:337
  62.1 10.4 %collective-permute-start.5 = (bf16[40,1024]{1,0:T(8,128)(2,1)S(1)}, bf16[40,1024]{1,0:T(8,128)(2,1)S(1)}, u32[]{:S(2)}, u32[]{:S(2)}) collective-permute-start(bf16[40,1024]{1,0:T(8,128)(2,1)S(1)} %wave_part.1.refs_0_), channel_id=1, source_target_pairs={{0,64},{32,96},{64,0},{96,32},{128,192},{160,224},{192,128},{224,1... | collective-permute-start | bytes 245768 | tf_op jit(solution)/shard_map/ppermute | solution.py:299
  65.5 7.8 %collective-permute-start.6 = (bf16[40,1024]{1,0:T(8,128)(2,1)S(1)}, bf16[40,1024]{1,0:T(8,128)(2,1)S(1)}, u32[]{:S(2)}, u32[]{:S(2)}) collective-permute-start(bf16[40,1024]{1,0:T(8,128)(2,1)S(1)} %wave_part.1.refs_0_), channel_id=1, source_target_pairs={{0,128},{32,160},{64,192},{96,224},{128,0},{160,32},{192,64},{224,... | collective-permute-start | bytes 245768 | tf_op jit(solution)/shard_map/ppermute | solution.py:299
  70.1 7.5 %collective-permute-start.7 = (bf16[40,1024]{1,0:T(8,128)(2,1)S(1)}, bf16[40,1024]{1,0:T(8,128)(2,1)S(1)}, u32[]{:S(2)}, u32[]{:S(2)}) collective-permute-start(bf16[40,1024]{1,0:T(8,128)(2,1)S(1)} %wave_part.1.refs_0_), channel_id=1, source_target_pairs={{0,192},{32,224},{64,128},{96,160},{128,64},{160,96},{192,0},{224,... | collective-permute-start | bytes 245768 | tf_op jit(solution)/shard_map/ppermute | solution.py:299

commit v3 on v2

--- a/solution.py
+++ b/solution.py
@@ -47,11 +47,9 @@
     product = index[:, None] * index[None, :] % N
     angle = product.astype(np.float32) * np.float32(2.0 * math.pi / N)
     scale = np.float32(1.0 / math.sqrt(N))
-    shape = (FACETS // 2, 2, 16, HALF)
-    return (
-        (np.cos(angle) * scale).astype(bf16).reshape(shape),
-        (np.sin(angle) * scale).astype(bf16).reshape(shape),
-    )
+    shape = (2, FACETS // 2, 2, 16, HALF)
+    pair = np.stack([np.cos(angle) * scale, np.sin(angle) * scale])
+    return pair.astype(bf16).reshape(shape)
 
 
 def tap_pair(shift):
@@ -119,8 +117,13 @@
     return jnp.concatenate([part[0] + sign * part[1], part[2] + sign * part[3]], axis=1)
 
 
-def regrouped(table_ref):
-    return jnp.concatenate([table_ref[:, h].reshape(256, HALF) for h in range(2)], axis=0)
+def plain(tables_ref, which):
+    return tables_ref[which].reshape(HALF, HALF)
+
+
+def regrouped(tables_ref, which):
+    parts = [tables_ref[which, :, h].reshape(256, HALF) for h in range(2)]
+    return jnp.concatenate(parts, axis=0)
 
 
 def split(pieces):
@@ -130,34 +133,20 @@
     )
 
 
-def forward_kernel(
-    margin_ref, image_ref, cos_ref, sin_ref,
-    out_ref, low_ref, high_ref, held_ref, cos_out, sin_out, image_sem, table_sems,
-):
+def forward_kernel(image_ref, tables_ref, out_ref, held_ref, tables_out, image_sem, table_sem):
     image_copy = pltpu.make_async_copy(image_ref.at[0], held_ref, image_sem)
+    tables_copy = pltpu.make_async_copy(tables_ref, tables_out, table_sem)
     image_copy.start()
-    copies = [
-        pltpu.make_async_copy(cos_ref, cos_out, table_sems.at[0]),
-        pltpu.make_async_copy(sin_ref, sin_out, table_sems.at[1]),
-    ]
-    for copy in copies:
-        copy.start()
+    tables_copy.start()
     image_copy.wait()
-    width = jnp.broadcast_to(margin_ref[0].astype(f32), (8, N))
-    line = lax.broadcasted_iota(jnp.int32, (8, N), 0)
-    low_ref[...] = jnp.where(line == 0, width, held_ref[24:, :])
-    high_ref[...] = jnp.where(line == 7, width, held_ref[:8, :])
     flat = held_ref[...].astype(bf16)
     left = quarters(flat[:, :HALF], flat[:, HALF:])
-    copies[0].wait()
-    real = whole(dot(left, cos_out[...].reshape(HALF, HALF)))
-    copies[1].wait()
-    imag = -whole(dot(left, sin_out[...].reshape(HALF, HALF)))
-    pack(real, imag, out_ref)
+    tables_copy.wait()
+    pack(whole(dot(left, plain(tables_out, 0))), -whole(dot(left, plain(tables_out, 1))), out_ref)
 
 
 def vis_kernel(
-    got_ref, cells_ref, gains_ref, seen_ref, dual_ref, cos_ref, sin_ref, dual_out, out_ref
+    got_ref, cells_ref, gains_ref, seen_ref, dual_ref, tables_ref, dual_out, out_ref
 ):
     turned = got_ref[...].reshape(512, 128).T
     left = quarters(
@@ -170,8 +159,8 @@
             ]
         )
     )
-    by_cos = whole(dot(left, regrouped(cos_ref)))
-    by_sin = whole(dot(left, regrouped(sin_ref)))
+    by_cos = whole(dot(left, regrouped(tables_ref, 0)))
+    by_sin = whole(dot(left, regrouped(tables_ref, 1)))
     grid = (by_cos[:32] + by_sin[32:], by_cos[32:] - by_sin[:32])
     stacked = jnp.concatenate(
         [part[:, 256 * t : 256 * t + 256] for part in grid for t in range(4)], axis=0
@@ -216,8 +205,8 @@
         axis=0,
     )
     left = quarters(held[:, :HALF], held[:, HALF:])
-    by_cos = whole(dot(left, cos_ref[...].reshape(HALF, HALF)))
-    by_sin = whole(dot(left, sin_ref[...].reshape(HALF, HALF)))
+    by_cos = whole(dot(left, plain(tables_ref, 0)))
+    by_sin = whole(dot(left, plain(tables_ref, 1)))
     pack(by_cos[:32] - by_sin[32:], by_sin[:32] + by_cos[32:], out_ref)
 
 
@@ -254,22 +243,22 @@
     square_ref[...] = (coef * coef)[:40].astype(bf16)
 
 
-def back_kernel(coef_ref, rows_ref, *refs):
-    total = sum(ref[...].astype(f32) for ref in refs[:-1])
+def join_kernel(parts_ref, out_ref):
+    out_ref[...] = jnp.sum(parts_ref[...].astype(f32), axis=0).astype(bf16)
+
+
+def back_kernel(coef_ref, rows_ref, parts_ref, out_ref):
+    total = jnp.sum(parts_ref[...].astype(f32), axis=0)
     factor = bound_level / jnp.maximum(jnp.sqrt(total), bound_level)
     mixed = exact_dot(rows_ref[0:40, :], coef_ref[0:40, :] * factor, ((0,), (0,)))
-    refs[-1][...] = filtered_columns(mixed[8:40], True)
-
-
-def join_kernel(*refs):
-    refs[-1][...] = sum(ref[...].astype(f32) for ref in refs[:-1]).astype(bf16)
-
-
-def final_kernel(got_ref, image_ref, wave_ref, cos_ref, sin_ref, out_ref):
+    out_ref[...] = filtered_columns(mixed[8:40], True)
+
+
+def final_kernel(got_ref, image_ref, wave_ref, tables_ref, out_ref):
     turned = got_ref[...].reshape(512, 128).T
     real = quarters(*split([turned[:32], turned[32:64]]))
     imag = quarters(*split([turned[64:96], turned[96:]]))
-    data = whole(dot(real, regrouped(cos_ref)) - dot(imag, regrouped(sin_ref)))
+    data = whole(dot(real, regrouped(tables_ref, 0)) - dot(imag, regrouped(tables_ref, 1)))
     total = data + wave_ref[...]
     out_ref[0] = jnp.maximum(image_ref[...] - tau_step * total, 0.0)
 
@@ -295,30 +284,24 @@
     return jax.ShapeDtypeStruct(dims, kind)
 
 
-def swapped(value, steps):
-    moved = [lax.ppermute(value, "chan", [(i, i ^ s) for i in range(CHANNELS)]) for s in steps]
-    return [value] + moved
-
-
 def local(image, margin, cells, weights, observed, dual_start):
-    cos_table, sin_table = (jnp.asarray(t) for t in fourier_tables())
+    tables = jnp.asarray(fourier_tables())
     chunks = shape((FACETS, 16, 128), bf16)
     squares = shape((40, N), bf16)
-    edge = shape((8, N), f32)
-    table = shape(cos_table.shape, bf16)
     up = [(i, i + 1) for i in range(FACETS - 1)]
     down = [(i + 1, i) for i in range(FACETS - 1)]
-    sent, low, high, held, cos_held, sin_held = call(
+    wide = jnp.broadcast_to(margin.astype(f32)[:, None], (1, N))
+    low = lax.ppermute(jnp.concatenate([wide, image[0, 25:]], axis=0), "slab", up)
+    high = lax.ppermute(jnp.concatenate([image[0, :7], wide], axis=0), "slab", down)
+    sent, held, tables_held = call(
         forward_kernel,
         "rows_out",
-        (chunks, edge, edge, shape((ROWS, N), f32), table, table),
-        margin, image, cos_table, sin_table,
-        specs=[in_smem] + [in_hbm] * 3,
-        scratch=[pltpu.SemaphoreType.DMA, pltpu.SemaphoreType.DMA((2,))],
-    )
-    got = lax.all_to_all(sent, "slab", 0, 0, tiled=True)
-    low = lax.ppermute(low, "slab", up)
-    high = lax.ppermute(high, "slab", down)
+        (chunks, shape((ROWS, N), f32), shape(tables.shape, bf16)),
+        image, tables,
+        specs=[in_hbm] * 2,
+        scratch=[pltpu.SemaphoreType.DMA, pltpu.SemaphoreType.DMA],
+    )
+    sent, low, high = lax.optimization_barrier((sent, low, high))
     coef, square, rows = call(
         wave_kernel,
         "wave_out",
@@ -326,21 +309,24 @@
         margin, held, low, high,
         specs=[in_smem] + [in_vmem] * 3,
     )
-    part = call(join_kernel, "wave_part", squares, *swapped(square, (1, 8, 9)))
+    got = lax.all_to_all(sent, "slab", 0, 0, tiled=True)
+    near = [[c, c + 1, c + 8, c + 9] for c in (0, 2, 4, 6)]
+    far = [[c, c + 2, c + 4, c + 6] for c in (0, 1, 8, 9)]
+    parts = lax.all_gather(square, "chan", axis_index_groups=near)
+    part = call(join_kernel, "wave_part", squares, parts)
     got, part = lax.optimization_barrier((got, part))
     dual, back = call(
         vis_kernel,
         "visibilities",
         (shape((2, 1, VIS), f32), chunks),
-        got, cells, weights, observed, dual_start, cos_held, sin_held,
+        got, cells, weights, observed, dual_start, tables_held,
     )
     returned = lax.all_to_all(back, "slab", 0, 0, tiled=True)
-    wave = call(
-        back_kernel, "wave_back", shape((ROWS, N), f32), coef, rows, *swapped(part, (2, 4, 6))
-    )
+    gathered = lax.all_gather(part, "chan", axis_index_groups=far)
+    wave = call(back_kernel, "wave_back", shape((ROWS, N), f32), coef, rows, gathered)
     fresh = call(
         final_kernel, "image_out", shape((1, ROWS, N), f32),
-        returned, held, wave, cos_held, sin_held,
+        returned, held, wave, tables_held,
     )
     return (fresh, dual)
 

time: 80 us -> 68.6 us (0.86)
  starting transfers between devices: 54.4 us -> 32.5 us
  blocking collectives: 0 us -> 20.1 us
  waiting for transfers between devices: 12 us -> 3.85 us
  local copies, waits for them, and re-layouts: 3.01 us -> 2.09 us
    all_gather x0 -> x2, blocking collectives: none -> 20.1 us  [the longest x1 12.7 us: local(): gathered = lax.all_gather(part, 'chan', axis_index_groups=far)]
    ppermute x8 -> x2, starting transfers between devices: 27 us -> 12.7 us  [the longest x1 6.66 us: local(): lax.ppermute(jnp.concatenate([image[0, :7], wide], axis=0), 'slab', down)]
    ppermute x8 -> x2, waiting for transfers between devices: 12 us -> 0.04 us  [the longest x1 0.04 us: local(): lax.ppermute(jnp.concatenate([image[0, :7], wide], axis=0), 'slab', down)]
    all_to_all x1, starting transfers between devices: 16.2 us -> 11.8 us  [local(): got = lax.all_to_all(sent, 'slab', 0, 0, tiled=True)]
    all_to_all x1, waiting for transfers between devices: 0.01 us -> 3.81 us  [local(): got = lax.all_to_all(sent, 'slab', 0, 0, tiled=True)]
    all_to_all x1, starting transfers between devices: 11.2 us -> 7.97 us  [local(): returned = lax.all_to_all(back, 'slab', 0, 0, tiled=True)]
    unnamed x14 -> x12, local copies, waits for them, and re-layouts: 3.01 us -> 1.24 us
    squeeze x0 -> x1, local copies, waits for them, and re-layouts: none -> 0.83 us  [local(): image[0, :7]]
  transfers between devices with their start and end apart: 10 -> 4, of which waited for: 6 -> 1; matrix products, arithmetic and copies ran while one was open for 0% -> 0% of each run, Pallas kernels for 2% -> 4%
where the time goes in v3:
time: 68.6 us; the launch traced here: 68.2 us
  starting transfers between devices  32.5 us (47%)
  blocking collectives  20.1 us (29%)
  Pallas kernels  8.3 us (12%)
  waiting for transfers between devices  3.85 us (6%)
  local copies, waits for them, and re-layouts  2.09 us (3%)
  between operations  1.4 us (2%)
    all_gather x1, blocking collectives, local(): gathered = lax.all_gather(part, 'chan', axis_index_groups=far)  12.7 us
    all_to_all x1, starting transfers between devices, local(): got = lax.all_to_all(sent, 'slab', 0, 0, tiled=True)  11.8 us
    pallas_call x6, Pallas kernels, call(): pl.pallas_call(kernel, out_shape=out_shape, in_specs=specs or [in_vmem] *...  8.3 us
    all_to_all x1, starting transfers between devices, local(): returned = lax.all_to_all(back, 'slab', 0, 0, tiled=True)  7.97 us
    all_gather x1, blocking collectives, local(): parts = lax.all_gather(square, 'chan', axis_index_groups=near)  7.35 us
    ppermute x1, starting transfers between devices, local(): lax.ppermute(jnp.concatenate([image[0, :7], wide], axis=0), 'slab', down)  6.66 us
    ppermute x1, starting transfers between devices, local(): lax.ppermute(jnp.concatenate([wide, image[0, 25:]], axis=0), 'slab', up)  6.09 us
    all_to_all x1, waiting for transfers between devices, local(): got = lax.all_to_all(sent, 'slab', 0, 0, tiled=True)  3.81 us
  transfers between devices with their start and end apart: 4, of which 1 were waited for; matrix products, arithmetic and copies ran while one was open for 0% of the time, Pallas kernels for 4%

profile of v3, /device:TPU:8, one launch (start us, length us, event | category | flops | bytes accessed | tf_op | source)
XLA Modules:
  0.0 68.2 jit_solution(3951520514993850921)
XLA Ops:
  1.3 0.0 copy-start.1
  1.3 0.8 %slice_bitcast_fusion = (f32[7,1024]{1,0:T(8,128)S(1)}, f32[7,1024]{1,0:T(8,128)S(1)}) fusion(f32[1,32,1024]{2,1,0:T(8,128)} %image_ref.1), kind=kLoop, calls=%fused_computation | loop fusion | bytes 114688 | tf_op jit(solution)/shard_map/squeeze | solution.py:295
  2.1 6.1 %collective-permute-start = (f32[8,1024]{1,0:T(8,128)S(1)}, f32[8,1024]{1,0:T(8,128)S(1)}, u32[]{:S(2)}, u32[]{:S(2)}) collective-permute-start(f32[8,1024]{1,0:T(8,128)S(1)} %concatenate.6), channel_id=1, source_target_pairs={{0,1},{1,2},{2,3},{3,4},{4,5},{5,6},{6,7},{7,8},{8,9},{9,10},{10,1... | collective-permute-start | bytes 98312 | tf_op jit(solution)/shard_map/ppermute | solution.py:294
  8.2 6.7 %collective-permute-start.1 = (f32[8,1024]{1,0:T(8,128)S(1)}, f32[8,1024]{1,0:T(8,128)S(1)}, u32[]{:S(2)}, u32[]{:S(2)}) collective-permute-start(f32[8,1024]{1,0:T(8,128)S(1)} %concatenate.7), channel_id=1, source_target_pairs={{1,0},{2,1},{3,2},{4,3},{5,4},{6,5},{7,6},{8,7},{9,8},{10,9},{11,1... | collective-permute-start | bytes 98312 | tf_op jit(solution)/shard_map/ppermute | solution.py:295
  14.9 0.0 copy-done.1
  14.9 0.0 copy-start
  14.9 1.2 %copy-done = bf16[2,16,2,16,512]{4,3,2,1,0:T(8,128)(2,1)S(1)} copy-done((bf16[2,16,2,16,512]{4,3,2,1,0:T(8,128)(2,1)S(1)}, bf16[2,16,2,16,512]{4,3,2,1,0:T(8,128)(2,1)}, u32[]{:S(2)}) %copy-start) | copy-done | bytes 1048600
  16.1 1.4 %rows_out.1 = (bf16[32,16,128]{2,1,0:T(8,128)(2,1)}, f32[32,1024]{1,0:T(8,128)S(1)}, bf16[2,16,2,16,512]{4,3,2,1,0:T(8,128)(2,1)S(1)}) custom-call(f32[1,32,1024]{2,1,0:T(8,128)S(1)} %copy-done.1, bf16[2,16,2,16,512]{4,3,2,1,0:T(8,128)(2,1)S(1)} %copy-done), custom_call_target="tpu_custom_call" | custom-call | tf_op jit(solution)/shard_map/rows_out/pallas_call | solution.py:272
  17.5 0.0 collective-permute-done.low_ref
  17.5 0.0 collective-permute-done.1.high_ref
  17.6 11.8 %all-to-all-start = ((bf16[32,16,128]{2,1,0:T(8,128)(2,1)}), bf16[32,16,128]{2,1,0:T(8,128)(2,1)S(1)}, u32[]{:S(2)}, u32[]{:S(2)}) async-start(bf16[32,16,128]{2,1,0:T(8,128)(2,1)} %get-tuple-element.16), calls=%async_computation | async-start | bytes 262144 | tf_op jit(solution)/shard_map/all_to_all | solution.py:312
  29.3 0.7 %wave_out.1 = (f32[48,1024]{1,0:T(8,128)S(1)}, bf16[40,1024]{1,0:T(8,128)(2,1)S(1)}, f32[48,48]{1,0:T(8,128)S(1)}) custom-call(s32[1]{0:T(128)S(6)} %copy.9.margin_ref, f32[32,1024]{1,0:T(8,128)S(1)} %get-tuple-element.17.image_ref, f32[8,1024]{1,0:T(8,128)S(1)} %collective-permute-done.low_ref, f32[8,1024]{1,0:T(8,128)S(1)} %collective-permute-done.1.high_ref), custom_call_target="tpu_custom_call" | custom-call | tf_op jit(solution)/shard_map/wave_out/pallas_call | solution.py:272
  30.1 7.3 %all-gather = bf16[160,1024]{1,0:T(8,128)(2,1)S(1)} all-gather(bf16[40,1024]{1,0:T(8,128)(2,1)S(1)} %get-tuple-element.20), channel_id=2, replica_groups={{0,32,256,288},{64,96,320,352},{128,160,384,416},{192,224,448,480},{1,3..., dimensions={0}, use_global_device_ids=true | all-gather | bytes 409600 | tf_op jit(solution)/shard_map/all_gather | solution.py:315
  37.4 0.0 copy-start.2
  37.4 0.0 copy-start.3
  37.4 0.0 copy-start.4
  37.4 0.0 copy-start.5
  37.5 3.8 %all-to-all-done.got_ref = bf16[32,16,128]{2,1,0:T(8,128)(2,1)S(1)} async-done(((bf16[32,16,128]{2,1,0:T(8,128)(2,1)}), bf16[32,16,128]{2,1,0:T(8,128)(2,1)S(1)}, u32[]{:S(2)}, u32[]{:S(2)}) %all-to-all-start) | async-done | bytes 131104 | tf_op jit(solution)/shard_map/all_to_all | solution.py:312
  41.3 0.0 copy-done.2
  41.3 0.0 copy-done.3
  41.3 0.0 copy-done.4
  41.3 0.0 copy-done.5
  41.3 4.5 %visibilities.1 = (f32[2,1,4096]{2,1,0:T(1,128)}, bf16[32,16,128]{2,1,0:T(8,128)(2,1)}) custom-call(bf16[32,16,128]{2,1,0:T(8,128)(2,1)S(1)} %all-to-all-done.got_ref, s32[1,4096]{1,0:T(1,128)S(1)} %copy-done.4, f32[1,4096]{1,0:T(1,128)S(1)} %copy-done.5, f32[2,1,4096]{2,1,0:T(1,128)S(1)} %copy-done.2, f32[2,1,4096]{2,1,0:T(1,128)S(1)} %copy-done.3, ...), custom_call_target="tpu_custom_call" | custom-call | tf_op jit(solution)/shard_map/visibilities/pallas_call | solution.py:272
  45.8 8.0 %all-to-all-start.1 = ((bf16[32,16,128]{2,1,0:T(8,128)(2,1)}), bf16[32,16,128]{2,1,0:T(8,128)(2,1)S(1)}, u32[]{:S(2)}, u32[]{:S(2)}) async-start(bf16[32,16,128]{2,1,0:T(8,128)(2,1)} %get-tuple-element.23), calls=%async_computation.1 | async-start | bytes 262144 | tf_op jit(solution)/shard_map/all_to_all | solution.py:324
  53.8 12.7 %all-gather.1 = bf16[160,1024]{1,0:T(8,128)(2,1)S(1)} all-gather(bf16[40,1024]{1,0:T(8,128)(2,1)S(1)} %wave_part.1), channel_id=3, replica_groups={{0,64,128,192},{32,96,160,224},{256,320,384,448},{288,352,416,480},{1,6..., dimensions={0}, use_global_device_ids=true | all-gather | bytes 409600 | tf_op jit(solution)/shard_map/all_gather | solution.py:325
  66.5 0.6 wave_back.1.wave_ref
  67.2 0.0 all-to-all-done.1.got_ref
  67.2 1.0 %image_out.1 = f32[1,32,1024]{2,1,0:T(8,128)} custom-call(bf16[32,16,128]{2,1,0:T(8,128)(2,1)S(1)} %all-to-all-done.1.got_ref, f32[32,1024]{1,0:T(8,128)S(1)} %get-tuple-element.17.image_ref, f32[32,1024]{1,0:T(8,128)S(1)} %wave_back.1.wave_ref, bf16[2,16,2,16,512]{4,3,2,1,0:T(8,128)(2,1)S(1)} %get-tuple-element.22.tables_ref), custom_call_target="tpu_custom_call" | custom-call | tf_op jit(solution)/shard_map/image_out/pallas_call | solution.py:272
  (3 shorter events, 0.1 us)
Async XLA Ops:
  1.3 13.6 %copy-start.1 = (f32[1,32,1024]{2,1,0:T(8,128)S(1)}, f32[1,32,1024]{2,1,0:T(8,128)}, u32[]{:S(2)}) copy-start(f32[1,32,1024]{2,1,0:T(8,128)} %image_ref.1) | copy-start | bytes 393220
  2.1 15.4 %collective-permute-start = (f32[8,1024]{1,0:T(8,128)S(1)}, f32[8,1024]{1,0:T(8,128)S(1)}, u32[]{:S(2)}, u32[]{:S(2)}) collective-permute-start(f32[8,1024]{1,0:T(8,128)S(1)} %concatenate.6), channel_id=1, source_target_pairs={{0,1},{1,2},{2,3},{3,4},{4,5},{5,6},{6,7},{7,8},{8,9},{9,10},{10,1... | collective-permute-start | bytes 98312 | tf_op jit(solution)/shard_map/ppermute | solution.py:294
  8.2 9.3 %collective-permute-start.1 = (f32[8,1024]{1,0:T(8,128)S(1)}, f32[8,1024]{1,0:T(8,128)S(1)}, u32[]{:S(2)}, u32[]{:S(2)}) collective-permute-start(f32[8,1024]{1,0:T(8,128)S(1)} %concatenate.7), channel_id=1, source_target_pairs={{1,0},{2,1},{3,2},{4,3},{5,4},{6,5},{7,6},{8,7},{9,8},{10,9},{11,1... | collective-permute-start | bytes 98312 | tf_op jit(solution)/shard_map/ppermute | solution.py:295
  14.9 1.2 %copy-start = (bf16[2,16,2,16,512]{4,3,2,1,0:T(8,128)(2,1)S(1)}, bf16[2,16,2,16,512]{4,3,2,1,0:T(8,128)(2,1)}, u32[]{:S(2)}) copy-start(bf16[2,16,2,16,512]{4,3,2,1,0:T(8,128)(2,1)} %constant.2.clone.tables_ref) | copy-start | bytes 3145732
  17.6 23.7 %all-to-all-start = ((bf16[32,16,128]{2,1,0:T(8,128)(2,1)}), bf16[32,16,128]{2,1,0:T(8,128)(2,1)S(1)}, u32[]{:S(2)}, u32[]{:S(2)}) async-start(bf16[32,16,128]{2,1,0:T(8,128)(2,1)} %get-tuple-element.16), calls=%async_computation | async-start | bytes 262144 | tf_op jit(solution)/shard_map/all_to_all | solution.py:312
  37.4 3.9 %copy-start.2 = (f32[2,1,4096]{2,1,0:T(1,128)S(1)}, f32[2,1,4096]{2,1,0:T(1,128)}, u32[]{:S(2)}) copy-start(f32[2,1,4096]{2,1,0:T(1,128)} %seen_ref.1) | copy-start | bytes 98308
  37.4 3.9 %copy-start.3 = (f32[2,1,4096]{2,1,0:T(1,128)S(1)}, f32[2,1,4096]{2,1,0:T(1,128)}, u32[]{:S(2)}) copy-start(f32[2,1,4096]{2,1,0:T(1,128)} %dual_ref.1) | copy-start | bytes 98308
  37.4 3.9 %copy-start.4 = (s32[1,4096]{1,0:T(1,128)S(1)}, s32[1,4096]{1,0:T(1,128)}, u32[]{:S(2)}) copy-start(s32[1,4096]{1,0:T(1,128)} %cells_ref.1) | copy-start | bytes 49156
  37.4 3.9 %copy-start.5 = (f32[1,4096]{1,0:T(1,128)S(1)}, f32[1,4096]{1,0:T(1,128)}, u32[]{:S(2)}) copy-start(f32[1,4096]{1,0:T(1,128)} %gains_ref.1) | copy-start | bytes 49156
  45.8 21.4 %all-to-all-start.1 = ((bf16[32,16,128]{2,1,0:T(8,128)(2,1)}), bf16[32,16,128]{2,1,0:T(8,128)(2,1)S(1)}, u32[]{:S(2)}, u32[]{:S(2)}) async-start(bf16[32,16,128]{2,1,0:T(8,128)(2,1)} %get-tuple-element.23), calls=%async_computation.1 | async-start | bytes 262144 | tf_op jit(solution)/shard_map/all_to_all | solution.py:324

commit v4 on v3

--- a/solution.py
+++ b/solution.py
@@ -311,7 +311,8 @@
     )
     got = lax.all_to_all(sent, "slab", 0, 0, tiled=True)
     near = [[c, c + 1, c + 8, c + 9] for c in (0, 2, 4, 6)]
-    far = [[c, c + 2, c + 4, c + 6] for c in (0, 1, 8, 9)]
+    beside = [[c, c + 2] for c in (0, 1, 4, 5, 8, 9, 12, 13)]
+    across = [[c, c + 4] for c in (0, 1, 2, 3, 8, 9, 10, 11)]
     parts = lax.all_gather(square, "chan", axis_index_groups=near)
     part = call(join_kernel, "wave_part", squares, parts)
     got, part = lax.optimization_barrier((got, part))
@@ -322,7 +323,9 @@
         got, cells, weights, observed, dual_start, tables_held,
     )
     returned = lax.all_to_all(back, "slab", 0, 0, tiled=True)
-    gathered = lax.all_gather(part, "chan", axis_index_groups=far)
+    parts = lax.all_gather(part, "chan", axis_index_groups=beside)
+    part = call(join_kernel, "wave_more", squares, parts)
+    gathered = lax.all_gather(part, "chan", axis_index_groups=across)
     wave = call(back_kernel, "wave_back", shape((ROWS, N), f32), coef, rows, gathered)
     fresh = call(
         final_kernel, "image_out", shape((1, ROWS, N), f32),

time: 68.6 us -> 67.8 us (0.988)
  blocking collectives: 20.1 us -> 19.1 us
    all_gather x1 -> x2, blocking collectives: 12.7 us -> 11.7 us  [the longest x1 6.62 us: local(): gathered = lax.all_gather(part, 'chan', axis_index_groups=across)]
    pallas_call x6 -> x7, Pallas kernels: 8.3 us -> 8.32 us  [call(): pl.pallas_call(kernel, out_shape=out_shape, in_specs=specs or [in_vmem] *...]
  transfers between devices with their start and end apart: 4 -> 4, of which waited for: 1 -> 2; matrix products, arithmetic and copies ran while one was open for 0% -> 0% of each run, Pallas kernels for 4% -> 4%
where the time goes in v4:
time: 67.8 us; the launch traced here: 67.3 us
  starting transfers between devices  32.5 us (48%)
  blocking collectives  19.1 us (28%)
  Pallas kernels  8.32 us (12%)
  waiting for transfers between devices  3.97 us (6%)
  local copies, waits for them, and re-layouts  2.09 us (3%)
  between operations  1.4 us (2%)
    all_to_all x1, starting transfers between devices, local(): got = lax.all_to_all(sent, 'slab', 0, 0, tiled=True)  11.8 us
    pallas_call x7, Pallas kernels, call(): pl.pallas_call(kernel, out_shape=out_shape, in_specs=specs or [in_vmem] *...  8.32 us
    all_to_all x1, starting transfers between devices, local(): returned = lax.all_to_all(back, 'slab', 0, 0, tiled=True)  7.97 us
    all_gather x1, blocking collectives, local(): parts = lax.all_gather(square, 'chan', axis_index_groups=near)  7.35 us
    ppermute x1, starting transfers between devices, local(): lax.ppermute(jnp.concatenate([image[0, :7], wide], axis=0), 'slab', down)  6.66 us
    all_gather x1, blocking collectives, local(): gathered = lax.all_gather(part, 'chan', axis_index_groups=across)  6.62 us
    ppermute x1, starting transfers between devices, local(): lax.ppermute(jnp.concatenate([wide, image[0, 25:]], axis=0), 'slab', up)  6.09 us
    all_gather x1, blocking collectives, local(): parts = lax.all_gather(part, 'chan', axis_index_groups=beside)  5.12 us
  transfers between devices with their start and end apart: 4, of which 2 were waited for; matrix products, arithmetic and copies ran while one was open for 0% of the time, Pallas kernels for 4%

profile of v4, /device:TPU:8, one launch (start us, length us, event | category | flops | bytes accessed | tf_op | source)
XLA Modules:
  0.0 67.3 jit_solution(13120707064339102757)
XLA Ops:
  1.3 0.0 copy-start.1
  1.3 0.8 %slice_bitcast_fusion = (f32[7,1024]{1,0:T(8,128)S(1)}, f32[7,1024]{1,0:T(8,128)S(1)}) fusion(f32[1,32,1024]{2,1,0:T(8,128)} %image_ref.1), kind=kLoop, calls=%fused_computation | loop fusion | bytes 114688 | tf_op jit(solution)/shard_map/squeeze | solution.py:295
  2.1 6.1 %collective-permute-start = (f32[8,1024]{1,0:T(8,128)S(1)}, f32[8,1024]{1,0:T(8,128)S(1)}, u32[]{:S(2)}, u32[]{:S(2)}) collective-permute-start(f32[8,1024]{1,0:T(8,128)S(1)} %concatenate.6), channel_id=1, source_target_pairs={{0,1},{1,2},{2,3},{3,4},{4,5},{5,6},{6,7},{7,8},{8,9},{9,10},{10,1... | collective-permute-start | bytes 98312 | tf_op jit(solution)/shard_map/ppermute | solution.py:294
  8.2 6.7 %collective-permute-start.1 = (f32[8,1024]{1,0:T(8,128)S(1)}, f32[8,1024]{1,0:T(8,128)S(1)}, u32[]{:S(2)}, u32[]{:S(2)}) collective-permute-start(f32[8,1024]{1,0:T(8,128)S(1)} %concatenate.7), channel_id=1, source_target_pairs={{1,0},{2,1},{3,2},{4,3},{5,4},{6,5},{7,6},{8,7},{9,8},{10,9},{11,1... | collective-permute-start | bytes 98312 | tf_op jit(solution)/shard_map/ppermute | solution.py:295
  14.9 0.0 copy-done.1
  14.9 0.0 copy-start
  14.9 1.2 %copy-done = bf16[2,16,2,16,512]{4,3,2,1,0:T(8,128)(2,1)S(1)} copy-done((bf16[2,16,2,16,512]{4,3,2,1,0:T(8,128)(2,1)S(1)}, bf16[2,16,2,16,512]{4,3,2,1,0:T(8,128)(2,1)}, u32[]{:S(2)}) %copy-start) | copy-done | bytes 1048600
  16.1 1.4 %rows_out.1 = (bf16[32,16,128]{2,1,0:T(8,128)(2,1)}, f32[32,1024]{1,0:T(8,128)S(1)}, bf16[2,16,2,16,512]{4,3,2,1,0:T(8,128)(2,1)S(1)}) custom-call(f32[1,32,1024]{2,1,0:T(8,128)S(1)} %copy-done.1, bf16[2,16,2,16,512]{4,3,2,1,0:T(8,128)(2,1)S(1)} %copy-done), custom_call_target="tpu_custom_call" | custom-call | tf_op jit(solution)/shard_map/rows_out/pallas_call | solution.py:272
  17.5 0.0 collective-permute-done.low_ref
  17.5 0.0 collective-permute-done.1.high_ref
  17.6 11.8 %all-to-all-start = ((bf16[32,16,128]{2,1,0:T(8,128)(2,1)}), bf16[32,16,128]{2,1,0:T(8,128)(2,1)S(1)}, u32[]{:S(2)}, u32[]{:S(2)}) async-start(bf16[32,16,128]{2,1,0:T(8,128)(2,1)} %get-tuple-element.16), calls=%async_computation | async-start | bytes 262144 | tf_op jit(solution)/shard_map/all_to_all | solution.py:312
  29.3 0.7 %wave_out.1 = (f32[48,1024]{1,0:T(8,128)S(1)}, bf16[40,1024]{1,0:T(8,128)(2,1)S(1)}, f32[48,48]{1,0:T(8,128)S(1)}) custom-call(s32[1]{0:T(128)S(6)} %copy.9.margin_ref, f32[32,1024]{1,0:T(8,128)S(1)} %get-tuple-element.17.image_ref, f32[8,1024]{1,0:T(8,128)S(1)} %collective-permute-done.low_ref, f32[8,1024]{1,0:T(8,128)S(1)} %collective-permute-done.1.high_ref), custom_call_target="tpu_custom_call" | custom-call | tf_op jit(solution)/shard_map/wave_out/pallas_call | solution.py:272
  30.1 7.3 %all-gather = bf16[160,1024]{1,0:T(8,128)(2,1)S(1)} all-gather(bf16[40,1024]{1,0:T(8,128)(2,1)S(1)} %get-tuple-element.20), channel_id=2, replica_groups={{0,32,256,288},{64,96,320,352},{128,160,384,416},{192,224,448,480},{1,3..., dimensions={0}, use_global_device_ids=true | all-gather | bytes 409600 | tf_op jit(solution)/shard_map/all_gather | solution.py:316
  37.4 0.0 copy-start.2
  37.4 0.0 copy-start.3
  37.4 0.0 copy-start.4
  37.4 0.0 copy-start.5
  37.5 3.8 %all-to-all-done.got_ref = bf16[32,16,128]{2,1,0:T(8,128)(2,1)S(1)} async-done(((bf16[32,16,128]{2,1,0:T(8,128)(2,1)}), bf16[32,16,128]{2,1,0:T(8,128)(2,1)S(1)}, u32[]{:S(2)}, u32[]{:S(2)}) %all-to-all-start) | async-done | bytes 131104 | tf_op jit(solution)/shard_map/all_to_all | solution.py:312
  41.3 0.0 copy-done.2
  41.3 0.0 copy-done.3
  41.3 0.0 copy-done.4
  41.3 0.0 copy-done.5
  41.3 4.5 %visibilities.1 = (f32[2,1,4096]{2,1,0:T(1,128)}, bf16[32,16,128]{2,1,0:T(8,128)(2,1)}) custom-call(bf16[32,16,128]{2,1,0:T(8,128)(2,1)S(1)} %all-to-all-done.got_ref, s32[1,4096]{1,0:T(1,128)S(1)} %copy-done.4, f32[1,4096]{1,0:T(1,128)S(1)} %copy-done.5, f32[2,1,4096]{2,1,0:T(1,128)S(1)} %copy-done.2, f32[2,1,4096]{2,1,0:T(1,128)S(1)} %copy-done.3, ...), custom_call_target="tpu_custom_call" | custom-call | tf_op jit(solution)/shard_map/visibilities/pallas_call | solution.py:272
  45.8 8.0 %all-to-all-start.1 = ((bf16[32,16,128]{2,1,0:T(8,128)(2,1)}), bf16[32,16,128]{2,1,0:T(8,128)(2,1)S(1)}, u32[]{:S(2)}, u32[]{:S(2)}) async-start(bf16[32,16,128]{2,1,0:T(8,128)(2,1)} %get-tuple-element.23), calls=%async_computation.1 | async-start | bytes 262144 | tf_op jit(solution)/shard_map/all_to_all | solution.py:325
  53.8 5.1 %all-gather.1 = bf16[80,1024]{1,0:T(8,128)(2,1)S(1)} all-gather(bf16[40,1024]{1,0:T(8,128)(2,1)S(1)} %wave_part.1), channel_id=3, replica_groups={{0,64},{32,96},{128,192},{160,224},{256,320},{288,352},{384,448},{416,4..., dimensions={0}, use_global_device_ids=true | all-gather | bytes 245760 | tf_op jit(solution)/shard_map/all_gather | solution.py:326
  58.9 6.6 %all-gather.2 = bf16[80,1024]{1,0:T(8,128)(2,1)S(1)} all-gather(bf16[40,1024]{1,0:T(8,128)(2,1)S(1)} %wave_more.1), channel_id=4, replica_groups={{0,128},{32,160},{64,192},{96,224},{256,384},{288,416},{320,448},{352,4..., dimensions={0}, use_global_device_ids=true | all-gather | bytes 245760 | tf_op jit(solution)/shard_map/all_gather | solution.py:328
  65.5 0.6 wave_back.1.wave_ref
  66.2 0.1 all-to-all-done.1.got_ref
  66.3 1.0 %image_out.1 = f32[1,32,1024]{2,1,0:T(8,128)} custom-call(bf16[32,16,128]{2,1,0:T(8,128)(2,1)S(1)} %all-to-all-done.1.got_ref, f32[32,1024]{1,0:T(8,128)S(1)} %get-tuple-element.17.image_ref, f32[32,1024]{1,0:T(8,128)S(1)} %wave_back.1.wave_ref, bf16[2,16,2,16,512]{4,3,2,1,0:T(8,128)(2,1)S(1)} %get-tuple-element.22.tables_ref), custom_call_target="tpu_custom_call" | custom-call | tf_op jit(solution)/shard_map/image_out/pallas_call | solution.py:272
  (4 shorter events, 0.1 us)
Async XLA Ops:
  1.3 13.6 %copy-start.1 = (f32[1,32,1024]{2,1,0:T(8,128)S(1)}, f32[1,32,1024]{2,1,0:T(8,128)}, u32[]{:S(2)}) copy-start(f32[1,32,1024]{2,1,0:T(8,128)} %image_ref.1) | copy-start | bytes 393220
  2.1 15.4 %collective-permute-start = (f32[8,1024]{1,0:T(8,128)S(1)}, f32[8,1024]{1,0:T(8,128)S(1)}, u32[]{:S(2)}, u32[]{:S(2)}) collective-permute-start(f32[8,1024]{1,0:T(8,128)S(1)} %concatenate.6), channel_id=1, source_target_pairs={{0,1},{1,2},{2,3},{3,4},{4,5},{5,6},{6,7},{7,8},{8,9},{9,10},{10,1... | collective-permute-start | bytes 98312 | tf_op jit(solution)/shard_map/ppermute | solution.py:294
  8.2 9.3 %collective-permute-start.1 = (f32[8,1024]{1,0:T(8,128)S(1)}, f32[8,1024]{1,0:T(8,128)S(1)}, u32[]{:S(2)}, u32[]{:S(2)}) collective-permute-start(f32[8,1024]{1,0:T(8,128)S(1)} %concatenate.7), channel_id=1, source_target_pairs={{1,0},{2,1},{3,2},{4,3},{5,4},{6,5},{7,6},{8,7},{9,8},{10,9},{11,1... | collective-permute-start | bytes 98312 | tf_op jit(solution)/shard_map/ppermute | solution.py:295
  14.9 1.2 %copy-start = (bf16[2,16,2,16,512]{4,3,2,1,0:T(8,128)(2,1)S(1)}, bf16[2,16,2,16,512]{4,3,2,1,0:T(8,128)(2,1)}, u32[]{:S(2)}) copy-start(bf16[2,16,2,16,512]{4,3,2,1,0:T(8,128)(2,1)} %constant.2.clone.tables_ref) | copy-start | bytes 3145732
  17.6 23.7 %all-to-all-start = ((bf16[32,16,128]{2,1,0:T(8,128)(2,1)}), bf16[32,16,128]{2,1,0:T(8,128)(2,1)S(1)}, u32[]{:S(2)}, u32[]{:S(2)}) async-start(bf16[32,16,128]{2,1,0:T(8,128)(2,1)} %get-tuple-element.16), calls=%async_computation | async-start | bytes 262144 | tf_op jit(solution)/shard_map/all_to_all | solution.py:312
  37.4 3.9 %copy-start.2 = (f32[2,1,4096]{2,1,0:T(1,128)S(1)}, f32[2,1,4096]{2,1,0:T(1,128)}, u32[]{:S(2)}) copy-start(f32[2,1,4096]{2,1,0:T(1,128)} %seen_ref.1) | copy-start | bytes 98308
  37.4 3.9 %copy-start.3 = (f32[2,1,4096]{2,1,0:T(1,128)S(1)}, f32[2,1,4096]{2,1,0:T(1,128)}, u32[]{:S(2)}) copy-start(f32[2,1,4096]{2,1,0:T(1,128)} %dual_ref.1) | copy-start | bytes 98308
  37.4 3.9 %copy-start.4 = (s32[1,4096]{1,0:T(1,128)S(1)}, s32[1,4096]{1,0:T(1,128)}, u32[]{:S(2)}) copy-start(s32[1,4096]{1,0:T(1,128)} %cells_ref.1) | copy-start | bytes 49156
  37.4 3.9 %copy-start.5 = (f32[1,4096]{1,0:T(1,128)S(1)}, f32[1,4096]{1,0:T(1,128)}, u32[]{:S(2)}) copy-start(f32[1,4096]{1,0:T(1,128)} %gains_ref.1) | copy-start | bytes 49156
  45.8 20.5 %all-to-all-start.1 = ((bf16[32,16,128]{2,1,0:T(8,128)(2,1)}), bf16[32,16,128]{2,1,0:T(8,128)(2,1)S(1)}, u32[]{:S(2)}, u32[]{:S(2)}) async-start(bf16[32,16,128]{2,1,0:T(8,128)(2,1)} %get-tuple-element.23), calls=%async_computation.1 | async-start | bytes 262144 | tf_op jit(solution)/shard_map/all_to_all | solution.py:325

commit v5 on v4

--- a/solution.py
+++ b/solution.py
@@ -146,8 +146,10 @@
 
 
 def vis_kernel(
-    got_ref, cells_ref, gains_ref, seen_ref, dual_ref, tables_ref, dual_out, out_ref
+    got_ref, parts_ref, cells_ref, gains_ref, seen_ref, dual_ref, tables_ref,
+    dual_out, out_ref, part_ref,
 ):
+    part_ref[...] = jnp.sum(parts_ref[...].astype(f32), axis=0).astype(bf16)
     turned = got_ref[...].reshape(512, 128).T
     left = quarters(
         *split(
@@ -165,11 +167,10 @@
     stacked = jnp.concatenate(
         [part[:, 256 * t : 256 * t + 256] for part in grid for t in range(4)], axis=0
     )
-    upper = stacked.astype(bf16)
-    lower = (stacked - upper.astype(f32)).astype(bf16)
-    lines = jnp.concatenate([upper, lower], axis=1)
-    cell_lane = lax.broadcasted_iota(jnp.int32, (256, STEP), 0)
+    lines = stacked.astype(bf16)
+    cell_lane = lax.broadcasted_iota(jnp.int32, (256, STEP), 0).astype(f32).astype(bf16)
     cell_line = lax.broadcasted_iota(jnp.int32, (128, STEP), 0)
+    one, zero = jnp.asarray(1.0, bf16), jnp.asarray(0.0, bf16)
     hold = jnp.zeros((256, 256), f32)
     for step in range(VIS // STEP):
         span = slice(STEP * step, STEP * (step + 1))
@@ -177,9 +178,9 @@
         lane = cell & 255
         line = ((cell >> 8) & 3) * 32 + (cell >> 10)
         gains = gains_ref[:, span]
-        here = jnp.where(cell_lane == lane, 1.0, 0.0).astype(bf16)
+        here = jnp.where(cell_lane == lane.astype(f32).astype(bf16), one, zero)
         chosen = cell_line == line
-        values = dot(lines, jnp.concatenate([here, here], axis=0))
+        values = dot(lines, here)
         spread = []
         for c in range(2):
             picked = jnp.sum(
@@ -231,13 +232,17 @@
 
 
 def wave_kernel(
-    margin_ref, image_ref, low_ref, high_ref, coef_ref, square_ref, rows_ref
+    margin_ref, image_ref, first_ref, second_ref, coef_ref, square_ref, rows_ref
 ):
-    above = jnp.broadcast_to(low_ref[0:1, 0:48], (48, 48))
-    below = jnp.broadcast_to(high_ref[7:8, 0:48], (48, 48))
+    first, second = first_ref[...], second_ref[...]
+    from_above = jnp.broadcast_to(first[0:1, :], (8, N)) > 0.0
+    low = jnp.where(from_above, first, second)
+    high = pltpu.roll(jnp.where(from_above, second, first), 7, 0)
+    above = jnp.broadcast_to(low[0:1, 0:48], (48, 48))
+    below = -jnp.broadcast_to(high[7:8, 0:48], (48, 48))
     rows = row_weights(above, margin_ref[0].astype(f32), below)
     rows_ref[...] = rows
-    extended = jnp.concatenate([low_ref[...], image_ref[...], high_ref[...]], axis=0)
+    extended = jnp.concatenate([low, image_ref[...], high], axis=0)
     coef = filtered_columns(exact_dot(rows, extended, ((1,), (0,))), False)
     coef_ref[...] = coef
     square_ref[...] = (coef * coef)[:40].astype(bf16)
@@ -247,20 +252,16 @@
     out_ref[...] = jnp.sum(parts_ref[...].astype(f32), axis=0).astype(bf16)
 
 
-def back_kernel(coef_ref, rows_ref, parts_ref, out_ref):
+def final_kernel(got_ref, image_ref, coef_ref, rows_ref, parts_ref, tables_ref, out_ref):
     total = jnp.sum(parts_ref[...].astype(f32), axis=0)
     factor = bound_level / jnp.maximum(jnp.sqrt(total), bound_level)
     mixed = exact_dot(rows_ref[0:40, :], coef_ref[0:40, :] * factor, ((0,), (0,)))
-    out_ref[...] = filtered_columns(mixed[8:40], True)
-
-
-def final_kernel(got_ref, image_ref, wave_ref, tables_ref, out_ref):
+    wave = filtered_columns(mixed[8:40], True)
     turned = got_ref[...].reshape(512, 128).T
     real = quarters(*split([turned[:32], turned[32:64]]))
     imag = quarters(*split([turned[64:96], turned[96:]]))
     data = whole(dot(real, regrouped(tables_ref, 0)) - dot(imag, regrouped(tables_ref, 1)))
-    total = data + wave_ref[...]
-    out_ref[0] = jnp.maximum(image_ref[...] - tau_step * total, 0.0)
+    out_ref[0] = jnp.maximum(image_ref[...] - tau_step * (data + wave), 0.0)
 
 
 in_vmem = pl.BlockSpec(memory_space=pltpu.VMEM)
@@ -288,11 +289,15 @@
     tables = jnp.asarray(fourier_tables())
     chunks = shape((FACETS, 16, 128), bf16)
     squares = shape((40, N), bf16)
-    up = [(i, i + 1) for i in range(FACETS - 1)]
-    down = [(i + 1, i) for i in range(FACETS - 1)]
+    inner = [(i, i ^ 1) for i in range(FACETS)]
+    outer = [(i, (i - 1 ^ 1) + 1) for i in range(1, FACETS - 1)]
     wide = jnp.broadcast_to(margin.astype(f32)[:, None], (1, N))
-    low = lax.ppermute(jnp.concatenate([wide, image[0, 25:]], axis=0), "slab", up)
-    high = lax.ppermute(jnp.concatenate([image[0, :7], wide], axis=0), "slab", down)
+    parity = lax.axis_index("slab") % 2
+    bottom = jnp.concatenate([wide, image[0, 25:]], axis=0)
+    top = jnp.concatenate([-wide, image[0, :7]], axis=0)
+    is_even = parity == 0
+    first = lax.ppermute(jnp.where(is_even, bottom, top), "slab", inner)
+    second = lax.ppermute(jnp.where(is_even, top, bottom), "slab", outer)
     sent, held, tables_held = call(
         forward_kernel,
         "rows_out",
@@ -301,12 +306,12 @@
         specs=[in_hbm] * 2,
         scratch=[pltpu.SemaphoreType.DMA, pltpu.SemaphoreType.DMA],
     )
-    sent, low, high = lax.optimization_barrier((sent, low, high))
+    sent, first, second = lax.optimization_barrier((sent, first, second))
     coef, square, rows = call(
         wave_kernel,
         "wave_out",
         (shape((48, N), f32), squares, shape((48, 48), f32)),
-        margin, held, low, high,
+        margin, held, first, second,
         specs=[in_smem] + [in_vmem] * 3,
     )
     got = lax.all_to_all(sent, "slab", 0, 0, tiled=True)
@@ -314,22 +319,19 @@
     beside = [[c, c + 2] for c in (0, 1, 4, 5, 8, 9, 12, 13)]
     across = [[c, c + 4] for c in (0, 1, 2, 3, 8, 9, 10, 11)]
     parts = lax.all_gather(square, "chan", axis_index_groups=near)
-    part = call(join_kernel, "wave_part", squares, parts)
-    got, part = lax.optimization_barrier((got, part))
-    dual, back = call(
+    dual, back, part = call(
         vis_kernel,
         "visibilities",
-        (shape((2, 1, VIS), f32), chunks),
-        got, cells, weights, observed, dual_start, tables_held,
+        (shape((2, 1, VIS), f32), chunks, squares),
+        got, parts, cells, weights, observed, dual_start, tables_held,
     )
     returned = lax.all_to_all(back, "slab", 0, 0, tiled=True)
     parts = lax.all_gather(part, "chan", axis_index_groups=beside)
     part = call(join_kernel, "wave_more", squares, parts)
     gathered = lax.all_gather(part, "chan", axis_index_groups=across)
-    wave = call(back_kernel, "wave_back", shape((ROWS, N), f32), coef, rows, gathered)
     fresh = call(
         final_kernel, "image_out", shape((1, ROWS, N), f32),
-        returned, held, wave, tables_held,
+        returned, held, coef, rows, gathered, tables_held,
     )
     return (fresh, dual)
 

time: 67.8 us -> 65 us (0.959)
  starting transfers between devices: 32.5 us -> 28.9 us
  waiting for transfers between devices: 3.97 us -> 5.87 us
  Pallas kernels: 8.32 us -> 7.01 us
    all_to_all x1, starting transfers between devices: 11.8 us -> 8.03 us  [local(): got = lax.all_to_all(sent, 'slab', 0, 0, tiled=True)]
    ppermute x2, waiting for transfers between devices: 0.04 us -> 1.52 us  [the longest x1 1.52 us: local(): first = lax.ppermute(jnp.where(is_even, bottom, top), 'slab', inner)]
    pallas_call x7 -> x5, Pallas kernels: 8.32 us -> 7.01 us  [call(): pl.pallas_call(kernel, out_shape=out_shape, in_specs=specs or [in_vmem] *...]
  transfers between devices with their start and end apart: 4 -> 4, of which waited for: 2 -> 3; matrix products, arithmetic and copies ran while one was open for 0% -> 0% of each run, Pallas kernels for 4% -> 3%
where the time goes in v5:
time: 65 us; the launch traced here: 64.6 us
  starting transfers between devices  28.9 us (44%)
  blocking collectives  19.4 us (30%)
  Pallas kernels  7.01 us (11%)
  waiting for transfers between devices  5.87 us (9%)
  local copies, waits for them, and re-layouts  2.08 us (3%)
  between operations  1.42 us (2%)
    ppermute x1, starting transfers between devices, local(): second = lax.ppermute(jnp.where(is_even, top, bottom), 'slab', outer)  10.8 us
    all_to_all x1, starting transfers between devices, local(): got = lax.all_to_all(sent, 'slab', 0, 0, tiled=True)  8.03 us
    all_gather x1, blocking collectives, local(): parts = lax.all_gather(square, 'chan', axis_index_groups=near)  7.61 us
    all_to_all x1, starting transfers between devices, local(): returned = lax.all_to_all(back, 'slab', 0, 0, tiled=True)  7.43 us
    pallas_call x5, Pallas kernels, call(): pl.pallas_call(kernel, out_shape=out_shape, in_specs=specs or [in_vmem] *...  7.01 us
    all_gather x1, blocking collectives, local(): gathered = lax.all_gather(part, 'chan', axis_index_groups=across)  6.62 us
    all_gather x1, blocking collectives, local(): parts = lax.all_gather(part, 'chan', axis_index_groups=beside)  5.12 us
    all_to_all x1, waiting for transfers between devices, local(): got = lax.all_to_all(sent, 'slab', 0, 0, tiled=True)  3.56 us
  transfers between devices with their start and end apart: 4, of which 3 were waited for; matrix products, arithmetic and copies ran while one was open for 0% of the time, Pallas kernels for 3%

profile of v5, /device:TPU:8, one launch (start us, length us, event | category | flops | bytes accessed | tf_op | source)
XLA Modules:
  0.0 64.6 jit_solution(6572368066175297667)
XLA Ops:
  1.3 0.0 copy-start.1
  1.3 0.8 %slice_bitcast_fusion.1 = (f32[7,1024]{1,0:T(8,128)S(1)}, f32[7,1024]{1,0:T(8,128)S(1)}) fusion(f32[1,32,1024]{2,1,0:T(8,128)} %image_ref.1), kind=kLoop, calls=%fused_computation.1 | loop fusion | bytes 114688 | tf_op jit(solution)/shard_map/squeeze | solution.py:296
  2.1 10.8 %collective-permute-start.1 = (f32[8,1024]{1,0:T(8,128)S(1)}, f32[8,1024]{1,0:T(8,128)S(1)}, u32[]{:S(2)}, u32[]{:S(2)}) collective-permute-start(f32[8,1024]{1,0:T(8,128)S(1)} %get-tuple-element.28), channel_id=1, source_target_pairs={{1,2},{2,1},{3,4},{4,3},{5,6},{6,5},{7,8},{8,7},{9,10},{10,9},{11,... | collective-permute-start | bytes 98312 | tf_op jit(solution)/shard_map/ppermute | solution.py:300
  13.0 2.6 %collective-permute-start = (f32[8,1024]{1,0:T(8,128)S(1)}, f32[8,1024]{1,0:T(8,128)S(1)}, u32[]{:S(2)}, u32[]{:S(2)}) collective-permute-start(f32[8,1024]{1,0:T(8,128)S(1)} %get-tuple-element.29), channel_id=1, source_target_pairs={{0,1},{1,0},{2,3},{3,2},{4,5},{5,4},{6,7},{7,6},{8,9},{9,8},{10,11... | collective-permute-start | bytes 98312 | tf_op jit(solution)/shard_map/ppermute | solution.py:299
  15.6 0.0 copy-done.1
  15.6 0.0 copy-start
  15.6 1.2 %copy-done = bf16[2,16,2,16,512]{4,3,2,1,0:T(8,128)(2,1)S(1)} copy-done((bf16[2,16,2,16,512]{4,3,2,1,0:T(8,128)(2,1)S(1)}, bf16[2,16,2,16,512]{4,3,2,1,0:T(8,128)(2,1)}, u32[]{:S(2)}) %copy-start) | copy-done | bytes 1048600
  16.8 1.4 %rows_out.1 = (bf16[32,16,128]{2,1,0:T(8,128)(2,1)}, f32[32,1024]{1,0:T(8,128)S(1)}, bf16[2,16,2,16,512]{4,3,2,1,0:T(8,128)(2,1)S(1)}) custom-call(f32[1,32,1024]{2,1,0:T(8,128)S(1)} %copy-done.1, bf16[2,16,2,16,512]{4,3,2,1,0:T(8,128)(2,1)S(1)} %copy-done), custom_call_target="tpu_custom_call" | custom-call | tf_op jit(solution)/shard_map/rows_out/pallas_call | solution.py:273
  18.2 0.0 collective-permute-done.1.second_ref
  18.2 1.5 %collective-permute-done.first_ref = f32[8,1024]{1,0:T(8,128)S(1)} collective-permute-done((f32[8,1024]{1,0:T(8,128)S(1)}, f32[8,1024]{1,0:T(8,128)S(1)}, u32[]{:S(2)}, u32[]{:S(2)}) %collective-permute-start) | collective-permute-done | bytes 32800 | tf_op jit(solution)/shard_map/ppermute | solution.py:299
  19.7 8.0 %all-to-all-start = ((bf16[32,16,128]{2,1,0:T(8,128)(2,1)}), bf16[32,16,128]{2,1,0:T(8,128)(2,1)S(1)}, u32[]{:S(2)}, u32[]{:S(2)}) async-start(bf16[32,16,128]{2,1,0:T(8,128)(2,1)} %get-tuple-element.15), calls=%async_computation | async-start | bytes 262144 | tf_op jit(solution)/shard_map/all_to_all | solution.py:317
  27.7 0.7 %wave_out.1 = (f32[48,1024]{1,0:T(8,128)S(1)}, bf16[40,1024]{1,0:T(8,128)(2,1)S(1)}, f32[48,48]{1,0:T(8,128)S(1)}) custom-call(s32[1]{0:T(128)S(6)} %copy.9.margin_ref, f32[32,1024]{1,0:T(8,128)S(1)} %get-tuple-element.16.image_ref, f32[8,1024]{1,0:T(8,128)S(1)} %collective-permute-done.first_ref, f32[8,1024]{1,0:T(8,128)S(1)} %collective-permute-done.1.second_ref), custom_call_target="tpu_custom_call" | custom-call | tf_op jit(solution)/shard_map/wave_out/pallas_call | solution.py:273
  28.5 0.0 copy-start.2
  28.5 0.0 copy-start.3
  28.5 0.0 copy-start.4
  28.5 0.0 copy-start.5
  28.5 7.6 %all-gather = bf16[160,1024]{1,0:T(8,128)(2,1)S(1)} all-gather(bf16[40,1024]{1,0:T(8,128)(2,1)S(1)} %get-tuple-element.19), channel_id=2, replica_groups={{0,32,256,288},{64,96,320,352},{128,160,384,416},{192,224,448,480},{1,3..., dimensions={0}, use_global_device_ids=true | all-gather | bytes 409600 | tf_op jit(solution)/shard_map/all_gather | solution.py:321
  36.1 3.6 %all-to-all-done.got_ref = bf16[32,16,128]{2,1,0:T(8,128)(2,1)S(1)} async-done(((bf16[32,16,128]{2,1,0:T(8,128)(2,1)}), bf16[32,16,128]{2,1,0:T(8,128)(2,1)S(1)}, u32[]{:S(2)}, u32[]{:S(2)}) %all-to-all-start) | async-done | bytes 131104 | tf_op jit(solution)/shard_map/all_to_all | solution.py:317
  39.7 0.0 copy-done.2
  39.7 0.0 copy-done.3
  39.7 0.0 copy-done.4
  39.7 0.0 copy-done.5
  39.7 3.5 %visibilities.1 = (f32[2,1,4096]{2,1,0:T(1,128)}, bf16[32,16,128]{2,1,0:T(8,128)(2,1)}, bf16[40,1024]{1,0:T(8,128)(2,1)S(1)}) custom-call(bf16[32,16,128]{2,1,0:T(8,128)(2,1)S(1)} %all-to-all-done.got_ref, bf16[4,40,1024]{2,1,0:T(8,128)(2,1)S(1)} %bitcast.9, s32[1,4096]{1,0:T(1,128)S(1)} %copy-done.4, f32[1,4096]{1,0:T(1,128)S(1)} %copy-done.5, ...), custom_call_target="tpu_custom_call" | custom-call | tf_op jit(solution)/shard_map/visibilities/pallas_call | solution.py:273
  43.2 7.4 %all-to-all-start.1 = ((bf16[32,16,128]{2,1,0:T(8,128)(2,1)}), bf16[32,16,128]{2,1,0:T(8,128)(2,1)S(1)}, u32[]{:S(2)}, u32[]{:S(2)}) async-start(bf16[32,16,128]{2,1,0:T(8,128)(2,1)} %get-tuple-element.21), calls=%async_computation.1 | async-start | bytes 262144 | tf_op jit(solution)/shard_map/all_to_all | solution.py:328
  50.7 5.1 %all-gather.1 = bf16[80,1024]{1,0:T(8,128)(2,1)S(1)} all-gather(bf16[40,1024]{1,0:T(8,128)(2,1)S(1)} %get-tuple-element.24), channel_id=3, replica_groups={{0,64},{32,96},{128,192},{160,224},{256,320},{288,352},{384,448},{416,4..., dimensions={0}, use_global_device_ids=true | all-gather | bytes 245760 | tf_op jit(solution)/shard_map/all_gather | solution.py:329
  55.8 6.6 %all-gather.2 = bf16[80,1024]{1,0:T(8,128)(2,1)S(1)} all-gather(bf16[40,1024]{1,0:T(8,128)(2,1)S(1)} %wave_more.1), channel_id=4, replica_groups={{0,128},{32,160},{64,192},{96,224},{256,384},{288,416},{320,448},{352,4..., dimensions={0}, use_global_device_ids=true | all-gather | bytes 245760 | tf_op jit(solution)/shard_map/all_gather | solution.py:331
  62.5 0.8 %all-to-all-done.1.got_ref = bf16[32,16,128]{2,1,0:T(8,128)(2,1)S(1)} async-done(((bf16[32,16,128]{2,1,0:T(8,128)(2,1)}), bf16[32,16,128]{2,1,0:T(8,128)(2,1)S(1)}, u32[]{:S(2)}, u32[]{:S(2)}) %all-to-all-start.1) | async-done | bytes 131104 | tf_op jit(solution)/shard_map/all_to_all | solution.py:328
  63.2 1.4 %image_out.1 = f32[1,32,1024]{2,1,0:T(8,128)} custom-call(bf16[32,16,128]{2,1,0:T(8,128)(2,1)S(1)} %all-to-all-done.1.got_ref, f32[32,1024]{1,0:T(8,128)S(1)} %get-tuple-element.16.image_ref, f32[48,1024]{1,0:T(8,128)S(1)} %get-tuple-element.22.coef_ref, f32[48,48]{1,0:T(8,128)S(1)} %get-tuple-element.23.rows_ref, bf16[2,40,1024]{2,1,0:T(8,128)(2,1)S(1)} %bitcast.10, ...), custom_call_target="tpu_custom_call" | custom-call | tf_op jit(solution)/shard_map/image_out/pallas_call | solution.py:273
  (2 shorter events, 0.0 us)
Async XLA Ops:
  1.3 14.3 %copy-start.1 = (f32[1,32,1024]{2,1,0:T(8,128)S(1)}, f32[1,32,1024]{2,1,0:T(8,128)}, u32[]{:S(2)}) copy-start(f32[1,32,1024]{2,1,0:T(8,128)} %image_ref.1) | copy-start | bytes 393220
  2.1 16.0 %collective-permute-start.1 = (f32[8,1024]{1,0:T(8,128)S(1)}, f32[8,1024]{1,0:T(8,128)S(1)}, u32[]{:S(2)}, u32[]{:S(2)}) collective-permute-start(f32[8,1024]{1,0:T(8,128)S(1)} %get-tuple-element.28), channel_id=1, source_target_pairs={{1,2},{2,1},{3,4},{4,3},{5,6},{6,5},{7,8},{8,7},{9,10},{10,9},{11,... | collective-permute-start | bytes 98312 | tf_op jit(solution)/shard_map/ppermute | solution.py:300
  13.0 6.7 %collective-permute-start = (f32[8,1024]{1,0:T(8,128)S(1)}, f32[8,1024]{1,0:T(8,128)S(1)}, u32[]{:S(2)}, u32[]{:S(2)}) collective-permute-start(f32[8,1024]{1,0:T(8,128)S(1)} %get-tuple-element.29), channel_id=1, source_target_pairs={{0,1},{1,0},{2,3},{3,2},{4,5},{5,4},{6,7},{7,6},{8,9},{9,8},{10,11... | collective-permute-start | bytes 98312 | tf_op jit(solution)/shard_map/ppermute | solution.py:299
  15.6 1.2 %copy-start = (bf16[2,16,2,16,512]{4,3,2,1,0:T(8,128)(2,1)S(1)}, bf16[2,16,2,16,512]{4,3,2,1,0:T(8,128)(2,1)}, u32[]{:S(2)}) copy-start(bf16[2,16,2,16,512]{4,3,2,1,0:T(8,128)(2,1)} %constant.20.clone.tables_ref) | copy-start | bytes 3145732
  19.7 20.0 %all-to-all-start = ((bf16[32,16,128]{2,1,0:T(8,128)(2,1)}), bf16[32,16,128]{2,1,0:T(8,128)(2,1)S(1)}, u32[]{:S(2)}, u32[]{:S(2)}) async-start(bf16[32,16,128]{2,1,0:T(8,128)(2,1)} %get-tuple-element.15), calls=%async_computation | async-start | bytes 262144 | tf_op jit(solution)/shard_map/all_to_all | solution.py:317
  28.5 11.2 %copy-start.2 = (f32[2,1,4096]{2,1,0:T(1,128)S(1)}, f32[2,1,4096]{2,1,0:T(1,128)}, u32[]{:S(2)}) copy-start(f32[2,1,4096]{2,1,0:T(1,128)} %seen_ref.1) | copy-start | bytes 98308
  28.5 11.2 %copy-start.3 = (f32[2,1,4096]{2,1,0:T(1,128)S(1)}, f32[2,1,4096]{2,1,0:T(1,128)}, u32[]{:S(2)}) copy-start(f32[2,1,4096]{2,1,0:T(1,128)} %dual_ref.1) | copy-start | bytes 98308
  28.5 11.2 %copy-start.4 = (s32[1,4096]{1,0:T(1,128)S(1)}, s32[1,4096]{1,0:T(1,128)}, u32[]{:S(2)}) copy-start(s32[1,4096]{1,0:T(1,128)} %cells_ref.1) | copy-start | bytes 49156
  28.5 11.2 %copy-start.5 = (f32[1,4096]{1,0:T(1,128)S(1)}, f32[1,4096]{1,0:T(1,128)}, u32[]{:S(2)}) copy-start(f32[1,4096]{1,0:T(1,128)} %gains_ref.1) | copy-start | bytes 49156
  43.2 20.0 %all-to-all-start.1 = ((bf16[32,16,128]{2,1,0:T(8,128)(2,1)}), bf16[32,16,128]{2,1,0:T(8,128)(2,1)S(1)}, u32[]{:S(2)}, u32[]{:S(2)}) async-start(bf16[32,16,128]{2,1,0:T(8,128)(2,1)} %get-tuple-element.21), calls=%async_computation.1 | async-start | bytes 262144 | tf_op jit(solution)/shard_map/all_to_all | solution.py:328

commit v6 on v5

--- a/solution.py
+++ b/solution.py
@@ -14,7 +14,7 @@
 FACETS = 32
 CHANNELS = 16
 VIS = 4096
-STEP = 512
+STEP = 256
 
 low_taps = (
     -0.010597401784997278,

time: 65 us -> 64.6 us (level)
  no operation moved by 1% of the time
where the time goes in v6:
time: 64.6 us; the launch traced here: 64.2 us
  starting transfers between devices  28.9 us (45%)
  blocking collectives  19.4 us (30%)
  Pallas kernels  6.6 us (10%)
  waiting for transfers between devices  5.87 us (9%)
  local copies, waits for them, and re-layouts  2.08 us (3%)
  between operations  1.42 us (2%)
    ppermute x1, starting transfers between devices, local(): second = lax.ppermute(jnp.where(is_even, top, bottom), 'slab', outer)  10.8 us
    all_to_all x1, starting transfers between devices, local(): got = lax.all_to_all(sent, 'slab', 0, 0, tiled=True)  8.03 us
    all_gather x1, blocking collectives, local(): parts = lax.all_gather(square, 'chan', axis_index_groups=near)  7.61 us
    all_to_all x1, starting transfers between devices, local(): returned = lax.all_to_all(back, 'slab', 0, 0, tiled=True)  7.44 us
    all_gather x1, blocking collectives, local(): gathered = lax.all_gather(part, 'chan', axis_index_groups=across)  6.62 us
    pallas_call x5, Pallas kernels, call(): pl.pallas_call(kernel, out_shape=out_shape, in_specs=specs or [in_vmem] *...  6.6 us
    all_gather x1, blocking collectives, local(): parts = lax.all_gather(part, 'chan', axis_index_groups=beside)  5.12 us
    all_to_all x1, waiting for transfers between devices, local(): got = lax.all_to_all(sent, 'slab', 0, 0, tiled=True)  3.56 us
  transfers between devices with their start and end apart: 4, of which 3 were waited for; matrix products, arithmetic and copies ran while one was open for 0% of the time, Pallas kernels for 3%

profile of v6, /device:TPU:8, one launch (start us, length us, event | category | flops | bytes accessed | tf_op | source)
XLA Modules:
  0.0 64.2 jit_solution(17199832201584691787)
XLA Ops:
  1.3 0.0 copy-start.1
  1.3 0.8 %slice_bitcast_fusion.1 = (f32[7,1024]{1,0:T(8,128)S(1)}, f32[7,1024]{1,0:T(8,128)S(1)}) fusion(f32[1,32,1024]{2,1,0:T(8,128)} %image_ref.1), kind=kLoop, calls=%fused_computation.1 | loop fusion | bytes 114688 | tf_op jit(solution)/shard_map/squeeze | solution.py:296
  2.1 10.8 %collective-permute-start.1 = (f32[8,1024]{1,0:T(8,128)S(1)}, f32[8,1024]{1,0:T(8,128)S(1)}, u32[]{:S(2)}, u32[]{:S(2)}) collective-permute-start(f32[8,1024]{1,0:T(8,128)S(1)} %get-tuple-element.28), channel_id=1, source_target_pairs={{1,2},{2,1},{3,4},{4,3},{5,6},{6,5},{7,8},{8,7},{9,10},{10,9},{11,... | collective-permute-start | bytes 98312 | tf_op jit(solution)/shard_map/ppermute | solution.py:300
  13.0 2.6 %collective-permute-start = (f32[8,1024]{1,0:T(8,128)S(1)}, f32[8,1024]{1,0:T(8,128)S(1)}, u32[]{:S(2)}, u32[]{:S(2)}) collective-permute-start(f32[8,1024]{1,0:T(8,128)S(1)} %get-tuple-element.29), channel_id=1, source_target_pairs={{0,1},{1,0},{2,3},{3,2},{4,5},{5,4},{6,7},{7,6},{8,9},{9,8},{10,11... | collective-permute-start | bytes 98312 | tf_op jit(solution)/shard_map/ppermute | solution.py:299
  15.6 0.0 copy-done.1
  15.6 0.0 copy-start
  15.6 1.2 %copy-done = bf16[2,16,2,16,512]{4,3,2,1,0:T(8,128)(2,1)S(1)} copy-done((bf16[2,16,2,16,512]{4,3,2,1,0:T(8,128)(2,1)S(1)}, bf16[2,16,2,16,512]{4,3,2,1,0:T(8,128)(2,1)}, u32[]{:S(2)}) %copy-start) | copy-done | bytes 1048600
  16.8 1.4 %rows_out.1 = (bf16[32,16,128]{2,1,0:T(8,128)(2,1)}, f32[32,1024]{1,0:T(8,128)S(1)}, bf16[2,16,2,16,512]{4,3,2,1,0:T(8,128)(2,1)S(1)}) custom-call(f32[1,32,1024]{2,1,0:T(8,128)S(1)} %copy-done.1, bf16[2,16,2,16,512]{4,3,2,1,0:T(8,128)(2,1)S(1)} %copy-done), custom_call_target="tpu_custom_call" | custom-call | tf_op jit(solution)/shard_map/rows_out/pallas_call | solution.py:273
  18.2 0.0 collective-permute-done.1.second_ref
  18.2 1.5 %collective-permute-done.first_ref = f32[8,1024]{1,0:T(8,128)S(1)} collective-permute-done((f32[8,1024]{1,0:T(8,128)S(1)}, f32[8,1024]{1,0:T(8,128)S(1)}, u32[]{:S(2)}, u32[]{:S(2)}) %collective-permute-start) | collective-permute-done | bytes 32800 | tf_op jit(solution)/shard_map/ppermute | solution.py:299
  19.7 8.0 %all-to-all-start = ((bf16[32,16,128]{2,1,0:T(8,128)(2,1)}), bf16[32,16,128]{2,1,0:T(8,128)(2,1)S(1)}, u32[]{:S(2)}, u32[]{:S(2)}) async-start(bf16[32,16,128]{2,1,0:T(8,128)(2,1)} %get-tuple-element.15), calls=%async_computation | async-start | bytes 262144 | tf_op jit(solution)/shard_map/all_to_all | solution.py:317
  27.7 0.7 %wave_out.1 = (f32[48,1024]{1,0:T(8,128)S(1)}, bf16[40,1024]{1,0:T(8,128)(2,1)S(1)}, f32[48,48]{1,0:T(8,128)S(1)}) custom-call(s32[1]{0:T(128)S(6)} %copy.9.margin_ref, f32[32,1024]{1,0:T(8,128)S(1)} %get-tuple-element.16.image_ref, f32[8,1024]{1,0:T(8,128)S(1)} %collective-permute-done.first_ref, f32[8,1024]{1,0:T(8,128)S(1)} %collective-permute-done.1.second_ref), custom_call_target="tpu_custom_call" | custom-call | tf_op jit(solution)/shard_map/wave_out/pallas_call | solution.py:273
  28.5 0.0 copy-start.2
  28.5 0.0 copy-start.3
  28.5 0.0 copy-start.4
  28.5 0.0 copy-start.5
  28.5 7.6 %all-gather = bf16[160,1024]{1,0:T(8,128)(2,1)S(1)} all-gather(bf16[40,1024]{1,0:T(8,128)(2,1)S(1)} %get-tuple-element.19), channel_id=2, replica_groups={{0,32,256,288},{64,96,320,352},{128,160,384,416},{192,224,448,480},{1,3..., dimensions={0}, use_global_device_ids=true | all-gather | bytes 409600 | tf_op jit(solution)/shard_map/all_gather | solution.py:321
  36.1 3.6 %all-to-all-done.got_ref = bf16[32,16,128]{2,1,0:T(8,128)(2,1)S(1)} async-done(((bf16[32,16,128]{2,1,0:T(8,128)(2,1)}), bf16[32,16,128]{2,1,0:T(8,128)(2,1)S(1)}, u32[]{:S(2)}, u32[]{:S(2)}) %all-to-all-start) | async-done | bytes 131104 | tf_op jit(solution)/shard_map/all_to_all | solution.py:317
  39.7 0.0 copy-done.2
  39.7 0.0 copy-done.3
  39.7 0.0 copy-done.4
  39.7 0.0 copy-done.5
  39.7 3.1 %visibilities.1 = (f32[2,1,4096]{2,1,0:T(1,128)}, bf16[32,16,128]{2,1,0:T(8,128)(2,1)}, bf16[40,1024]{1,0:T(8,128)(2,1)S(1)}) custom-call(bf16[32,16,128]{2,1,0:T(8,128)(2,1)S(1)} %all-to-all-done.got_ref, bf16[4,40,1024]{2,1,0:T(8,128)(2,1)S(1)} %bitcast.9, s32[1,4096]{1,0:T(1,128)S(1)} %copy-done.4, f32[1,4096]{1,0:T(1,128)S(1)} %copy-done.5, ...), custom_call_target="tpu_custom_call" | custom-call | tf_op jit(solution)/shard_map/visibilities/pallas_call | solution.py:273
  42.8 7.4 %all-to-all-start.1 = ((bf16[32,16,128]{2,1,0:T(8,128)(2,1)}), bf16[32,16,128]{2,1,0:T(8,128)(2,1)S(1)}, u32[]{:S(2)}, u32[]{:S(2)}) async-start(bf16[32,16,128]{2,1,0:T(8,128)(2,1)} %get-tuple-element.21), calls=%async_computation.1 | async-start | bytes 262144 | tf_op jit(solution)/shard_map/all_to_all | solution.py:328
  50.3 5.1 %all-gather.1 = bf16[80,1024]{1,0:T(8,128)(2,1)S(1)} all-gather(bf16[40,1024]{1,0:T(8,128)(2,1)S(1)} %get-tuple-element.24), channel_id=3, replica_groups={{0,64},{32,96},{128,192},{160,224},{256,320},{288,352},{384,448},{416,4..., dimensions={0}, use_global_device_ids=true | all-gather | bytes 245760 | tf_op jit(solution)/shard_map/all_gather | solution.py:329
  55.4 6.6 %all-gather.2 = bf16[80,1024]{1,0:T(8,128)(2,1)S(1)} all-gather(bf16[40,1024]{1,0:T(8,128)(2,1)S(1)} %wave_more.1), channel_id=4, replica_groups={{0,128},{32,160},{64,192},{96,224},{256,384},{288,416},{320,448},{352,4..., dimensions={0}, use_global_device_ids=true | all-gather | bytes 245760 | tf_op jit(solution)/shard_map/all_gather | solution.py:331
  62.1 0.8 %all-to-all-done.1.got_ref = bf16[32,16,128]{2,1,0:T(8,128)(2,1)S(1)} async-done(((bf16[32,16,128]{2,1,0:T(8,128)(2,1)}), bf16[32,16,128]{2,1,0:T(8,128)(2,1)S(1)}, u32[]{:S(2)}, u32[]{:S(2)}) %all-to-all-start.1) | async-done | bytes 131104 | tf_op jit(solution)/shard_map/all_to_all | solution.py:328
  62.8 1.4 %image_out.1 = f32[1,32,1024]{2,1,0:T(8,128)} custom-call(bf16[32,16,128]{2,1,0:T(8,128)(2,1)S(1)} %all-to-all-done.1.got_ref, f32[32,1024]{1,0:T(8,128)S(1)} %get-tuple-element.16.image_ref, f32[48,1024]{1,0:T(8,128)S(1)} %get-tuple-element.22.coef_ref, f32[48,48]{1,0:T(8,128)S(1)} %get-tuple-element.23.rows_ref, bf16[2,40,1024]{2,1,0:T(8,128)(2,1)S(1)} %bitcast.10, ...), custom_call_target="tpu_custom_call" | custom-call | tf_op jit(solution)/shard_map/image_out/pallas_call | solution.py:273
  (2 shorter events, 0.0 us)
Async XLA Ops:
  1.3 14.3 %copy-start.1 = (f32[1,32,1024]{2,1,0:T(8,128)S(1)}, f32[1,32,1024]{2,1,0:T(8,128)}, u32[]{:S(2)}) copy-start(f32[1,32,1024]{2,1,0:T(8,128)} %image_ref.1) | copy-start | bytes 393220
  2.1 16.0 %collective-permute-start.1 = (f32[8,1024]{1,0:T(8,128)S(1)}, f32[8,1024]{1,0:T(8,128)S(1)}, u32[]{:S(2)}, u32[]{:S(2)}) collective-permute-start(f32[8,1024]{1,0:T(8,128)S(1)} %get-tuple-element.28), channel_id=1, source_target_pairs={{1,2},{2,1},{3,4},{4,3},{5,6},{6,5},{7,8},{8,7},{9,10},{10,9},{11,... | collective-permute-start | bytes 98312 | tf_op jit(solution)/shard_map/ppermute | solution.py:300
  13.0 6.7 %collective-permute-start = (f32[8,1024]{1,0:T(8,128)S(1)}, f32[8,1024]{1,0:T(8,128)S(1)}, u32[]{:S(2)}, u32[]{:S(2)}) collective-permute-start(f32[8,1024]{1,0:T(8,128)S(1)} %get-tuple-element.29), channel_id=1, source_target_pairs={{0,1},{1,0},{2,3},{3,2},{4,5},{5,4},{6,7},{7,6},{8,9},{9,8},{10,11... | collective-permute-start | bytes 98312 | tf_op jit(solution)/shard_map/ppermute | solution.py:299
  15.6 1.2 %copy-start = (bf16[2,16,2,16,512]{4,3,2,1,0:T(8,128)(2,1)S(1)}, bf16[2,16,2,16,512]{4,3,2,1,0:T(8,128)(2,1)}, u32[]{:S(2)}) copy-start(bf16[2,16,2,16,512]{4,3,2,1,0:T(8,128)(2,1)} %constant.20.clone.tables_ref) | copy-start | bytes 3145732
  19.7 20.0 %all-to-all-start = ((bf16[32,16,128]{2,1,0:T(8,128)(2,1)}), bf16[32,16,128]{2,1,0:T(8,128)(2,1)S(1)}, u32[]{:S(2)}, u32[]{:S(2)}) async-start(bf16[32,16,128]{2,1,0:T(8,128)(2,1)} %get-tuple-element.15), calls=%async_computation | async-start | bytes 262144 | tf_op jit(solution)/shard_map/all_to_all | solution.py:317
  28.5 11.2 %copy-start.2 = (f32[2,1,4096]{2,1,0:T(1,128)S(1)}, f32[2,1,4096]{2,1,0:T(1,128)}, u32[]{:S(2)}) copy-start(f32[2,1,4096]{2,1,0:T(1,128)} %seen_ref.1) | copy-start | bytes 98308
  28.5 11.2 %copy-start.3 = (f32[2,1,4096]{2,1,0:T(1,128)S(1)}, f32[2,1,4096]{2,1,0:T(1,128)}, u32[]{:S(2)}) copy-start(f32[2,1,4096]{2,1,0:T(1,128)} %dual_ref.1) | copy-start | bytes 98308
  28.5 11.2 %copy-start.4 = (s32[1,4096]{1,0:T(1,128)S(1)}, s32[1,4096]{1,0:T(1,128)}, u32[]{:S(2)}) copy-start(s32[1,4096]{1,0:T(1,128)} %cells_ref.1) | copy-start | bytes 49156
  28.5 11.2 %copy-start.5 = (f32[1,4096]{1,0:T(1,128)S(1)}, f32[1,4096]{1,0:T(1,128)}, u32[]{:S(2)}) copy-start(f32[1,4096]{1,0:T(1,128)} %gains_ref.1) | copy-start | bytes 49156
  42.8 20.0 %all-to-all-start.1 = ((bf16[32,16,128]{2,1,0:T(8,128)(2,1)}), bf16[32,16,128]{2,1,0:T(8,128)(2,1)S(1)}, u32[]{:S(2)}, u32[]{:S(2)}) async-start(bf16[32,16,128]{2,1,0:T(8,128)(2,1)} %get-tuple-element.21), calls=%async_computation.1 | async-start | bytes 262144 | tf_op jit(solution)/shard_map/all_to_all | solution.py:328

commit v7 on v6

--- a/solution.py
+++ b/solution.py
@@ -133,16 +133,10 @@
     )
 
 
-def forward_kernel(image_ref, tables_ref, out_ref, held_ref, tables_out, image_sem, table_sem):
-    image_copy = pltpu.make_async_copy(image_ref.at[0], held_ref, image_sem)
-    tables_copy = pltpu.make_async_copy(tables_ref, tables_out, table_sem)
-    image_copy.start()
-    tables_copy.start()
-    image_copy.wait()
-    flat = held_ref[...].astype(bf16)
+def forward_kernel(image_ref, tables_ref, out_ref):
+    flat = image_ref[0].astype(bf16)
     left = quarters(flat[:, :HALF], flat[:, HALF:])
-    tables_copy.wait()
-    pack(whole(dot(left, plain(tables_out, 0))), -whole(dot(left, plain(tables_out, 1))), out_ref)
+    pack(whole(dot(left, plain(tables_ref, 0))), -whole(dot(left, plain(tables_ref, 1))), out_ref)
 
 
 def vis_kernel(
@@ -242,7 +236,7 @@
     below = -jnp.broadcast_to(high[7:8, 0:48], (48, 48))
     rows = row_weights(above, margin_ref[0].astype(f32), below)
     rows_ref[...] = rows
-    extended = jnp.concatenate([low, image_ref[...], high], axis=0)
+    extended = jnp.concatenate([low, image_ref[0], high], axis=0)
     coef = filtered_columns(exact_dot(rows, extended, ((1,), (0,))), False)
     coef_ref[...] = coef
     square_ref[...] = (coef * coef)[:40].astype(bf16)
@@ -261,7 +255,7 @@
     real = quarters(*split([turned[:32], turned[32:64]]))
     imag = quarters(*split([turned[64:96], turned[96:]]))
     data = whole(dot(real, regrouped(tables_ref, 0)) - dot(imag, regrouped(tables_ref, 1)))
-    out_ref[0] = jnp.maximum(image_ref[...] - tau_step * (data + wave), 0.0)
+    out_ref[0] = jnp.maximum(image_ref[0] - tau_step * (data + wave), 0.0)
 
 
 in_vmem = pl.BlockSpec(memory_space=pltpu.VMEM)
@@ -298,20 +292,13 @@
     is_even = parity == 0
     first = lax.ppermute(jnp.where(is_even, bottom, top), "slab", inner)
     second = lax.ppermute(jnp.where(is_even, top, bottom), "slab", outer)
-    sent, held, tables_held = call(
-        forward_kernel,
-        "rows_out",
-        (chunks, shape((ROWS, N), f32), shape(tables.shape, bf16)),
-        image, tables,
-        specs=[in_hbm] * 2,
-        scratch=[pltpu.SemaphoreType.DMA, pltpu.SemaphoreType.DMA],
-    )
+    sent = call(forward_kernel, "rows_out", chunks, image, tables)
     sent, first, second = lax.optimization_barrier((sent, first, second))
     coef, square, rows = call(
         wave_kernel,
         "wave_out",
         (shape((48, N), f32), squares, shape((48, 48), f32)),
-        margin, held, first, second,
+        margin, image, first, second,
         specs=[in_smem] + [in_vmem] * 3,
     )
     got = lax.all_to_all(sent, "slab", 0, 0, tiled=True)
@@ -323,7 +310,7 @@
         vis_kernel,
         "visibilities",
         (shape((2, 1, VIS), f32), chunks, squares),
-        got, parts, cells, weights, observed, dual_start, tables_held,
+        got, parts, cells, weights, observed, dual_start, tables,
     )
     returned = lax.all_to_all(back, "slab", 0, 0, tiled=True)
     parts = lax.all_gather(part, "chan", axis_index_groups=beside)
@@ -331,7 +318,7 @@
     gathered = lax.all_gather(part, "chan", axis_index_groups=across)
     fresh = call(
         final_kernel, "image_out", shape((1, ROWS, N), f32),
-        returned, held, coef, rows, gathered, tables_held,
+        returned, image, coef, rows, gathered, tables,
     )
     return (fresh, dual)
 

time: 64.6 us -> 64.6 us (level)
  no operation moved by 1% of the time
where the time goes in v7:
time: 64.6 us; the launch traced here: 64.2 us
  starting transfers between devices  28.9 us (45%)
  blocking collectives  19.4 us (30%)
  Pallas kernels  6.37 us (10%)
  waiting for transfers between devices  6.02 us (9%)
  local copies, waits for them, and re-layouts  2.08 us (3%)
  between operations  1.42 us (2%)
    ppermute x1, starting transfers between devices, local(): second = lax.ppermute(jnp.where(is_even, top, bottom), 'slab', outer)  10.8 us
    all_to_all x1, starting transfers between devices, local(): got = lax.all_to_all(sent, 'slab', 0, 0, tiled=True)  7.83 us
    all_gather x1, blocking collectives, local(): parts = lax.all_gather(square, 'chan', axis_index_groups=near)  7.71 us
    all_to_all x1, starting transfers between devices, local(): returned = lax.all_to_all(back, 'slab', 0, 0, tiled=True)  7.64 us
    all_gather x1, blocking collectives, local(): gathered = lax.all_gather(part, 'chan', axis_index_groups=across)  6.62 us
    pallas_call x5, Pallas kernels, call(): pl.pallas_call(kernel, out_shape=out_shape, in_specs=specs or [in_vmem] *...  6.37 us
    all_gather x1, blocking collectives, local(): parts = lax.all_gather(part, 'chan', axis_index_groups=beside)  5.12 us
    all_to_all x1, waiting for transfers between devices, local(): got = lax.all_to_all(sent, 'slab', 0, 0, tiled=True)  3.46 us
  transfers between devices with their start and end apart: 4, of which 3 were waited for; matrix products, arithmetic and copies ran while one was open for 0% of the time, Pallas kernels for 3%

profile of v7, /device:TPU:8, one launch (start us, length us, event | category | flops | bytes accessed | tf_op | source)
XLA Modules:
  0.0 64.2 jit_solution(7682936833311350112)
XLA Ops:
  1.3 0.0 copy-start.2
  1.3 0.8 %slice_bitcast_fusion.1 = (f32[7,1024]{1,0:T(8,128)S(1)}, f32[7,1024]{1,0:T(8,128)S(1)}) fusion(f32[1,32,1024]{2,1,0:T(8,128)} %image_ref.5), kind=kLoop, calls=%fused_computation.1 | loop fusion | bytes 114688 | tf_op jit(solution)/shard_map/squeeze | solution.py:290
  2.1 10.8 %collective-permute-start.1 = (f32[8,1024]{1,0:T(8,128)S(1)}, f32[8,1024]{1,0:T(8,128)S(1)}, u32[]{:S(2)}, u32[]{:S(2)}) collective-permute-start(f32[8,1024]{1,0:T(8,128)S(1)} %get-tuple-element.22), channel_id=1, source_target_pairs={{1,2},{2,1},{3,4},{4,3},{5,6},{6,5},{7,8},{8,7},{9,10},{10,9},{11,... | collective-permute-start | bytes 98312 | tf_op jit(solution)/shard_map/ppermute | solution.py:294
  13.0 2.6 %collective-permute-start = (f32[8,1024]{1,0:T(8,128)S(1)}, f32[8,1024]{1,0:T(8,128)S(1)}, u32[]{:S(2)}, u32[]{:S(2)}) collective-permute-start(f32[8,1024]{1,0:T(8,128)S(1)} %get-tuple-element.23), channel_id=1, source_target_pairs={{0,1},{1,0},{2,3},{3,2},{4,5},{5,4},{6,7},{7,6},{8,9},{9,8},{10,11... | collective-permute-start | bytes 98312 | tf_op jit(solution)/shard_map/ppermute | solution.py:293
  15.6 0.0 copy-done.2
  15.6 0.0 copy-start
  15.6 1.2 %copy-done = bf16[2,16,2,16,512]{4,3,2,1,0:T(8,128)(2,1)S(1)} copy-done((bf16[2,16,2,16,512]{4,3,2,1,0:T(8,128)(2,1)S(1)}, bf16[2,16,2,16,512]{4,3,2,1,0:T(8,128)(2,1)}, u32[]{:S(2)}) %copy-start) | copy-done | bytes 1048600
  16.8 0.0 copy-start.1
  16.8 1.1 %rows_out.1 = bf16[32,16,128]{2,1,0:T(8,128)(2,1)} custom-call(f32[1,32,1024]{2,1,0:T(8,128)S(1)} %copy-done.2, bf16[2,16,2,16,512]{4,3,2,1,0:T(8,128)(2,1)S(1)} %copy-done), custom_call_target="tpu_custom_call" | custom-call | tf_op jit(solution)/shard_map/rows_out/pallas_call | solution.py:267
  17.9 0.0 collective-permute-done.1.second_ref
  17.9 1.8 %collective-permute-done.first_ref = f32[8,1024]{1,0:T(8,128)S(1)} collective-permute-done((f32[8,1024]{1,0:T(8,128)S(1)}, f32[8,1024]{1,0:T(8,128)S(1)}, u32[]{:S(2)}, u32[]{:S(2)}) %collective-permute-start) | collective-permute-done | bytes 32800 | tf_op jit(solution)/shard_map/ppermute | solution.py:293
  19.7 7.8 %all-to-all-start = ((bf16[32,16,128]{2,1,0:T(8,128)(2,1)}), bf16[32,16,128]{2,1,0:T(8,128)(2,1)S(1)}, u32[]{:S(2)}, u32[]{:S(2)}) async-start(bf16[32,16,128]{2,1,0:T(8,128)(2,1)} %rows_out.1), calls=%async_computation | async-start | bytes 262144 | tf_op jit(solution)/shard_map/all_to_all | solution.py:304
  27.5 0.7 %wave_out.1 = (f32[48,1024]{1,0:T(8,128)S(1)}, bf16[40,1024]{1,0:T(8,128)(2,1)S(1)}, f32[48,48]{1,0:T(8,128)S(1)}) custom-call(s32[1]{0:T(128)S(6)} %copy.9.margin_ref, f32[1,32,1024]{2,1,0:T(8,128)S(1)} %copy-done.2, f32[8,1024]{1,0:T(8,128)S(1)} %collective-permute-done.first_ref, f32[8,1024]{1,0:T(8,128)S(1)} %collective-permute-done.1.second_ref), custom_call_target="tpu_custom_call" | custom-call | tf_op jit(solution)/shard_map/wave_out/pallas_call | solution.py:267
  28.3 0.0 copy-start.3
  28.3 0.0 copy-start.4
  28.3 0.0 copy-start.5
  28.3 0.0 copy-start.6
  28.3 7.7 %all-gather = bf16[160,1024]{1,0:T(8,128)(2,1)S(1)} all-gather(bf16[40,1024]{1,0:T(8,128)(2,1)S(1)} %get-tuple-element.14), channel_id=2, replica_groups={{0,32,256,288},{64,96,320,352},{128,160,384,416},{192,224,448,480},{1,3..., dimensions={0}, use_global_device_ids=true | all-gather | bytes 409600 | tf_op jit(solution)/shard_map/all_gather | solution.py:308
  36.0 3.5 %all-to-all-done.got_ref = bf16[32,16,128]{2,1,0:T(8,128)(2,1)S(1)} async-done(((bf16[32,16,128]{2,1,0:T(8,128)(2,1)}), bf16[32,16,128]{2,1,0:T(8,128)(2,1)S(1)}, u32[]{:S(2)}, u32[]{:S(2)}) %all-to-all-start) | async-done | bytes 131104 | tf_op jit(solution)/shard_map/all_to_all | solution.py:304
  39.5 0.0 copy-done.1
  39.5 0.0 copy-done.3
  39.5 0.0 copy-done.4
  39.5 0.0 copy-done.5
  39.5 0.0 copy-done.6
  39.5 3.1 %visibilities.1 = (f32[2,1,4096]{2,1,0:T(1,128)}, bf16[32,16,128]{2,1,0:T(8,128)(2,1)}, bf16[40,1024]{1,0:T(8,128)(2,1)S(1)}) custom-call(bf16[32,16,128]{2,1,0:T(8,128)(2,1)S(1)} %all-to-all-done.got_ref, bf16[4,40,1024]{2,1,0:T(8,128)(2,1)S(1)} %bitcast.9, s32[1,4096]{1,0:T(1,128)S(1)} %copy-done.5, f32[1,4096]{1,0:T(1,128)S(1)} %copy-done.6, ...), custom_call_target="tpu_custom_call" | custom-call | tf_op jit(solution)/shard_map/visibilities/pallas_call | solution.py:267
  42.6 7.6 %all-to-all-start.1 = ((bf16[32,16,128]{2,1,0:T(8,128)(2,1)}), bf16[32,16,128]{2,1,0:T(8,128)(2,1)S(1)}, u32[]{:S(2)}, u32[]{:S(2)}) async-start(bf16[32,16,128]{2,1,0:T(8,128)(2,1)} %get-tuple-element.15), calls=%async_computation.1 | async-start | bytes 262144 | tf_op jit(solution)/shard_map/all_to_all | solution.py:315
  50.3 5.1 %all-gather.1 = bf16[80,1024]{1,0:T(8,128)(2,1)S(1)} all-gather(bf16[40,1024]{1,0:T(8,128)(2,1)S(1)} %get-tuple-element.18), channel_id=3, replica_groups={{0,64},{32,96},{128,192},{160,224},{256,320},{288,352},{384,448},{416,4..., dimensions={0}, use_global_device_ids=true | all-gather | bytes 245760 | tf_op jit(solution)/shard_map/all_gather | solution.py:316
  55.4 6.6 %all-gather.2 = bf16[80,1024]{1,0:T(8,128)(2,1)S(1)} all-gather(bf16[40,1024]{1,0:T(8,128)(2,1)S(1)} %wave_more.1), channel_id=4, replica_groups={{0,128},{32,160},{64,192},{96,224},{256,384},{288,416},{320,448},{352,4..., dimensions={0}, use_global_device_ids=true | all-gather | bytes 245760 | tf_op jit(solution)/shard_map/all_gather | solution.py:318
  62.1 0.8 %all-to-all-done.1.got_ref = bf16[32,16,128]{2,1,0:T(8,128)(2,1)S(1)} async-done(((bf16[32,16,128]{2,1,0:T(8,128)(2,1)}), bf16[32,16,128]{2,1,0:T(8,128)(2,1)S(1)}, u32[]{:S(2)}, u32[]{:S(2)}) %all-to-all-start.1) | async-done | bytes 131104 | tf_op jit(solution)/shard_map/all_to_all | solution.py:315
  62.8 1.4 %image_out.1 = f32[1,32,1024]{2,1,0:T(8,128)} custom-call(bf16[32,16,128]{2,1,0:T(8,128)(2,1)S(1)} %all-to-all-done.1.got_ref, f32[1,32,1024]{2,1,0:T(8,128)S(1)} %copy-done.2, f32[48,1024]{1,0:T(8,128)S(1)} %get-tuple-element.16.coef_ref, f32[48,48]{1,0:T(8,128)S(1)} %get-tuple-element.17.rows_ref, bf16[2,40,1024]{2,1,0:T(8,128)(2,1)S(1)} %bitcast.10, ...), custom_call_target="tpu_custom_call" | custom-call | tf_op jit(solution)/shard_map/image_out/pallas_call | solution.py:267
  (2 shorter events, 0.0 us)
Async XLA Ops:
  1.3 14.3 %copy-start.2 = (f32[1,32,1024]{2,1,0:T(8,128)S(1)}, f32[1,32,1024]{2,1,0:T(8,128)}, u32[]{:S(2)}) copy-start(f32[1,32,1024]{2,1,0:T(8,128)} %image_ref.5) | copy-start | bytes 393220
  2.1 15.8 %collective-permute-start.1 = (f32[8,1024]{1,0:T(8,128)S(1)}, f32[8,1024]{1,0:T(8,128)S(1)}, u32[]{:S(2)}, u32[]{:S(2)}) collective-permute-start(f32[8,1024]{1,0:T(8,128)S(1)} %get-tuple-element.22), channel_id=1, source_target_pairs={{1,2},{2,1},{3,4},{4,3},{5,6},{6,5},{7,8},{8,7},{9,10},{10,9},{11,... | collective-permute-start | bytes 98312 | tf_op jit(solution)/shard_map/ppermute | solution.py:294
  13.0 6.7 %collective-permute-start = (f32[8,1024]{1,0:T(8,128)S(1)}, f32[8,1024]{1,0:T(8,128)S(1)}, u32[]{:S(2)}, u32[]{:S(2)}) collective-permute-start(f32[8,1024]{1,0:T(8,128)S(1)} %get-tuple-element.23), channel_id=1, source_target_pairs={{0,1},{1,0},{2,3},{3,2},{4,5},{5,4},{6,7},{7,6},{8,9},{9,8},{10,11... | collective-permute-start | bytes 98312 | tf_op jit(solution)/shard_map/ppermute | solution.py:293
  15.6 1.2 %copy-start = (bf16[2,16,2,16,512]{4,3,2,1,0:T(8,128)(2,1)S(1)}, bf16[2,16,2,16,512]{4,3,2,1,0:T(8,128)(2,1)}, u32[]{:S(2)}) copy-start(bf16[2,16,2,16,512]{4,3,2,1,0:T(8,128)(2,1)} %constant.20.clone.tables_ref) | copy-start | bytes 3145732
  16.8 22.7 %copy-start.1 = (bf16[2,16,2,16,512]{4,3,2,1,0:T(8,128)(2,1)S(1)}, bf16[2,16,2,16,512]{4,3,2,1,0:T(8,128)(2,1)}, u32[]{:S(2)}) copy-start(bf16[2,16,2,16,512]{4,3,2,1,0:T(8,128)(2,1)} %constant.20.clone.tables_ref) | copy-start | bytes 3145732
  19.7 19.8 %all-to-all-start = ((bf16[32,16,128]{2,1,0:T(8,128)(2,1)}), bf16[32,16,128]{2,1,0:T(8,128)(2,1)S(1)}, u32[]{:S(2)}, u32[]{:S(2)}) async-start(bf16[32,16,128]{2,1,0:T(8,128)(2,1)} %rows_out.1), calls=%async_computation | async-start | bytes 262144 | tf_op jit(solution)/shard_map/all_to_all | solution.py:304
  28.3 11.2 %copy-start.3 = (f32[2,1,4096]{2,1,0:T(1,128)S(1)}, f32[2,1,4096]{2,1,0:T(1,128)}, u32[]{:S(2)}) copy-start(f32[2,1,4096]{2,1,0:T(1,128)} %seen_ref.1) | copy-start | bytes 98308
  28.3 11.2 %copy-start.4 = (f32[2,1,4096]{2,1,0:T(1,128)S(1)}, f32[2,1,4096]{2,1,0:T(1,128)}, u32[]{:S(2)}) copy-start(f32[2,1,4096]{2,1,0:T(1,128)} %dual_ref.1) | copy-start | bytes 98308
  28.3 11.2 %copy-start.5 = (s32[1,4096]{1,0:T(1,128)S(1)}, s32[1,4096]{1,0:T(1,128)}, u32[]{:S(2)}) copy-start(s32[1,4096]{1,0:T(1,128)} %cells_ref.1) | copy-start | bytes 49156
  28.3 11.2 %copy-start.6 = (f32[1,4096]{1,0:T(1,128)S(1)}, f32[1,4096]{1,0:T(1,128)}, u32[]{:S(2)}) copy-start(f32[1,4096]{1,0:T(1,128)} %gains_ref.1) | copy-start | bytes 49156
  42.6 20.2 %all-to-all-start.1 = ((bf16[32,16,128]{2,1,0:T(8,128)(2,1)}), bf16[32,16,128]{2,1,0:T(8,128)(2,1)S(1)}, u32[]{:S(2)}, u32[]{:S(2)}) async-start(bf16[32,16,128]{2,1,0:T(8,128)(2,1)} %get-tuple-element.15), calls=%async_computation.1 | async-start | bytes 262144 | tf_op jit(solution)/shard_map/all_to_all | solution.py:315
